TPU v7x, 32 devices: a whole 2x2x4 slice. The times are simulated.
32 devices in a mesh: grp: 4 (over x, core), gx: 2 (over y), gy: 4 (over z).
Axes of the slice: x: 2, y: 2, z: 4, core: 2. Of those that a mesh axis runs over, the one named last changes fastest.
Arguments:
- flow_fields: float32 [4, 32, 4, 512], P('grp', None, 'gx', 'gy'), may hold values from -4 to 4
- level_set: float32 [4, 64, 8, 1024], P('grp', None, 'gx', 'gy'), may hold values from -9 to 9
- band_tiles: int32 [8, 2, 64], P(None, 'gx', 'gy'), may hold values 0 or 1
- nozzle_phase: int32 [8, 1024], P('gx', 'gy'), may hold values from 0 to 2
Outputs:
- flow_next: float32 [4, 32, 4, 512], P('grp', None, 'gx', 'gy')
All inputs are finite; a program needn't handle non-finite values. No bound on the sum of `band_tiles` on one device may be relied on, other than what follows from the above.
Results may differ from a plain program's by a relative error of at most 0.0003.
Values sent between devices are 32-bit elements; how exact they have to be, the bound alone decides.
A program may use at most 64 MiB of HBM per device.

v0:
```python
import jax
import jax.numpy as jnp
from jax import lax
from jax.sharding import PartitionSpec as P

SWEEPS = 3


WENO_EPS = 1e-06
STEP_FINE = 0.3
STEP_FLOW = 0.2
SURFACE = 6.0
SPREAD = 1.5
IMPLICIT = 0.5


def extended(block, sides, width):
    for axis, dim in sides:
        count = lax.axis_size(axis)
        forward = [(i, i + 1) for i in range(count - 1)]
        forward.append((count - 1, 0))
        backward = [(target, source) for source, target in forward]
        low = lax.ppermute(
            lax.slice_in_dim(block, block.shape[dim] - width, None, axis=dim), axis, forward
        )
        high = lax.ppermute(lax.slice_in_dim(block, 0, width, axis=dim), axis, backward)
        block = jnp.concatenate([low, block, high], axis=dim)
    return block


def weno_side(diff_one, diff_two, diff_three, diff_four, diff_five):
    cand_one = diff_one / 3.0 - 7.0 * diff_two / 6.0 + 11.0 * diff_three / 6.0
    cand_two = -diff_two / 6.0 + 5.0 * diff_three / 6.0 + diff_four / 3.0
    cand_three = diff_three / 3.0 + 5.0 * diff_four / 6.0 - diff_five / 6.0
    curve_one = diff_one - 2.0 * diff_two + diff_three
    slope_one = diff_one - 4.0 * diff_two + 3.0 * diff_three
    smooth_one = 13.0 / 12.0 * curve_one * curve_one + 0.25 * slope_one * slope_one
    curve_two = diff_two - 2.0 * diff_three + diff_four
    slope_two = diff_two - diff_four
    smooth_two = 13.0 / 12.0 * curve_two * curve_two + 0.25 * slope_two * slope_two
    curve_three = diff_three - 2.0 * diff_four + diff_five
    slope_three = 3.0 * diff_three - 4.0 * diff_four + diff_five
    smooth_three = 13.0 / 12.0 * curve_three * curve_three + 0.25 * slope_three * slope_three
    weight_one = 0.1 / ((WENO_EPS + smooth_one) * (WENO_EPS + smooth_one))
    weight_two = 0.6 / ((WENO_EPS + smooth_two) * (WENO_EPS + smooth_two))
    weight_three = 0.3 / ((WENO_EPS + smooth_three) * (WENO_EPS + smooth_three))
    return (weight_one * cand_one + weight_two * cand_two + weight_three * cand_three) / (
        weight_one + weight_two + weight_three
    )


def section_rate(padded, speeds, plane_rim):
    plane_count = padded.shape[0] - 2 * plane_rim
    row_count = padded.shape[1] - 6
    col_count = padded.shape[2] - 6

    def sample(offset, direction):
        if direction == 0:
            return padded[
                3 + offset : 3 + offset + plane_count, 3 : 3 + row_count, 3 : 3 + col_count
            ]
        if direction == 1:
            return padded[
                plane_rim : plane_rim + plane_count,
                3 + offset : 3 + offset + row_count,
                3 : 3 + col_count,
            ]
        return padded[
            plane_rim : plane_rim + plane_count,
            3 : 3 + row_count,
            3 + offset : 3 + offset + col_count,
        ]

    summed = jnp.zeros((plane_count, row_count, col_count), jnp.float32)
    for direction in range(3):
        differences = [
            sample(offset + 1, direction) - sample(offset, direction) for offset in range(-3, 3)
        ]
        minus_side = weno_side(
            differences[0], differences[1], differences[2], differences[3], differences[4]
        )
        plus_side = weno_side(
            differences[5], differences[4], differences[3], differences[2], differences[1]
        )
        upwind = jnp.where(speeds[direction] >= 0.0, minus_side, plus_side)
        summed = summed - speeds[direction] * upwind
    return summed


def refine(coarse):
    plane_count, height, breadth = coarse.shape
    spread_out = jnp.broadcast_to(
        coarse[:, None, :, None, :, None], (plane_count, 2, height, 2, breadth, 2)
    )
    return spread_out.reshape(2 * plane_count, 2 * height, 2 * breadth)


def coarsen(fine_field):
    plane_count, height, breadth = fine_field.shape
    blocks = fine_field.reshape(plane_count // 2, 2, height // 2, 2, breadth // 2, 2)
    return jnp.sum(blocks, axis=(1, 3, 5)) * 0.125


def band_cells(tile_flags):
    planes, height, breadth = tile_flags.shape
    spread_out = jnp.broadcast_to(
        tile_flags[:, None, :, None, :, None], (planes, 8, height, 4, breadth, 16)
    )
    return spread_out.reshape(planes * 8, height * 4, breadth * 16)


def with_nozzle(banded, phases):
    inflow = jnp.where(phases == 2, 1.5, jnp.where(phases == 1, -1.5, banded[0]))
    return jnp.concatenate([inflow[None], banded[1:]], axis=0)


def surface_finish(normal_x, normal_y, normal_z, curvature, surface_level):
    delta_peak = jnp.exp(-surface_level * surface_level / (2.0 * SPREAD * SPREAD)) / (
        SPREAD * 2.5066282746310002
    )
    strength = SURFACE * curvature * delta_peak
    fraction = 0.5 + 0.5 * jnp.tanh(surface_level / SPREAD)
    return jnp.stack(
        [
            coarsen(normal_x * strength),
            coarsen(normal_y * strength),
            coarsen(normal_z * strength),
            coarsen(fraction),
        ]
    )


def surface_slab(padded):
    grad_x = (padded[1:-1, 2:, 1:-1] - padded[1:-1, :-2, 1:-1]) * 0.5
    grad_y = (padded[1:-1, 1:-1, 2:] - padded[1:-1, 1:-1, :-2]) * 0.5
    grad_z = (padded[2:, 1:-1, 1:-1] - padded[:-2, 1:-1, 1:-1]) * 0.5
    inverse = 1.0 / jnp.sqrt(grad_x * grad_x + grad_y * grad_y + grad_z * grad_z + 1.0)
    normal_x = grad_x * inverse
    normal_y = grad_y * inverse
    normal_z = grad_z * inverse
    curvature = (normal_x[1:-1, 2:, 1:-1] - normal_x[1:-1, :-2, 1:-1]) * 0.5
    curvature = curvature + (normal_y[1:-1, 1:-1, 2:] - normal_y[1:-1, 1:-1, :-2]) * 0.5
    curvature = curvature + (normal_z[2:, 1:-1, 1:-1] - normal_z[:-2, 1:-1, 1:-1]) * 0.5
    return surface_finish(
        normal_x[1:-1, 1:-1, 1:-1],
        normal_y[1:-1, 1:-1, 1:-1],
        normal_z[1:-1, 1:-1, 1:-1],
        curvature,
        padded[2:-2, 2:-2, 2:-2],
    )


def centered(padded, direction):
    if direction == 0:
        middle = padded[:, 1:-1, 1:-1]
        return (jnp.roll(middle, -1, 0) - jnp.roll(middle, 1, 0)) * 0.5
    if direction == 1:
        return (padded[:, 2:, 1:-1] - padded[:, :-2, 1:-1]) * 0.5
    return (padded[:, 1:-1, 2:] - padded[:, 1:-1, :-2]) * 0.5


def predictor(padded_fields, component):
    moving = lax.dynamic_index_in_dim(padded_fields, component, 0, keepdims=False)
    inner_u = padded_fields[0, :, 1:-1, 1:-1]
    inner_v = padded_fields[1, :, 1:-1, 1:-1]
    inner_w = padded_fields[2, :, 1:-1, 1:-1]
    advect = -(
        inner_w * centered(moving, 0)
        + inner_u * centered(moving, 1)
        + inner_v * centered(moving, 2)
    )
    pressure = padded_fields[3]
    gradients = jnp.stack([centered(pressure, 1), centered(pressure, 2), centered(pressure, 0)])
    pushed = lax.dynamic_index_in_dim(gradients, component, 0, keepdims=False)
    return moving[:, 1:-1, 1:-1] + STEP_FLOW * (advect - pushed)


def sweep_once(padded, source):
    middle = padded[:, 1:-1, 1:-1]
    beside_all = (
        padded[:, 2:, 1:-1] + padded[:, :-2, 1:-1] + padded[:, 1:-1, 2:] + padded[:, 1:-1, :-2]
    )
    beside_all = beside_all + jnp.roll(middle, -1, 0) + jnp.roll(middle, 1, 0)
    return (source + IMPLICIT * beside_all) / (1.0 + 6.0 * IMPLICIT)


def spread_surface(level_set, band_tiles, nozzle_phase, inner_fields, is_level, group):
    fine_all = level_set[0]
    initial = lax.psum_scatter(
        jnp.where(is_level, fine_all, jnp.zeros_like(fine_all)),
        "grp",
        scatter_dimension=0,
        tiled=True,
    )
    coarse_planes = inner_fields.shape[1] // 4
    flow_slab = lax.dynamic_slice_in_dim(inner_fields, group * coarse_planes, coarse_planes, 1)
    speeds = (refine(flow_slab[2]), refine(flow_slab[0]), refine(flow_slab[1]))

    def run_section(current, keep_weight, blend_weight):
        padded = extended(current, (("grp", 0), ("gx", 1), ("gy", 2)), 3)
        return keep_weight * initial + blend_weight * (
            current + STEP_FINE * section_rate(padded, speeds, 3)
        )

    first_section = run_section(initial, 0.0, 1.0)
    second_section = run_section(first_section, 0.75, 0.25)
    third_section = run_section(second_section, 1.0 / 3.0, 2.0 / 3.0)
    tile_planes = band_tiles.shape[0] // 4
    tiles_here = lax.dynamic_slice_in_dim(band_tiles, group * tile_planes, tile_planes, 0)
    banded = jnp.where(band_cells(tiles_here) == 1, third_section, initial)
    shaped = jnp.where(group == 0, with_nozzle(banded, nozzle_phase), banded)
    surface_pad = extended(shaped, (("grp", 0), ("gx", 1), ("gy", 2)), 2)
    quarter = surface_slab(surface_pad)
    received = lax.all_to_all(quarter, "grp", split_axis=0, concat_axis=1, tiled=True)
    return (received, received[0])


def on_device(flow_fields, level_set, band_tiles, nozzle_phase):
    group = lax.axis_index("grp")
    component = jnp.minimum(group, 2)
    is_level = group == 3
    gathered = lax.all_gather(flow_fields, "grp", axis=0, tiled=True)
    padded_fields = extended(gathered, (("gx", 2), ("gy", 3)), 1)
    source = predictor(padded_fields, component)
    inner_fields = padded_fields[:, :, 1:-1, 1:-1]
    received, fraction = spread_surface(
        level_set, band_tiles, nozzle_phase, inner_fields, is_level, group
    )
    pushed = received[0]
    relaxed = source
    for sweep_number in range(SWEEPS):
        padded = extended(relaxed, (("gx", 1), ("gy", 2)), 1)
        relaxed = sweep_once(padded, source)
    updated = relaxed + STEP_FLOW * pushed
    result = jnp.where(is_level, fraction, updated)
    return result[None]


def solution(mesh):
    placed = (
        P("grp", None, "gx", "gy"),
        P("grp", None, "gx", "gy"),
        P(None, "gx", "gy"),
        P("gx", "gy"),
    )
    return jax.shard_map(
        on_device, mesh=mesh, in_specs=placed, out_specs=P("grp", None, "gx", "gy"), check_vma=False
    )
```

profile of v0, /device:TPU:0, one launch (start us, length us, event | category | flops | bytes accessed | tf_op | source)
XLA Modules:
  0.0 189.7 jit_solution(3335985181046255501)
XLA Ops:
  6.5 1.7 fusion
  9.0 6.5 %all_gather.3 = f32[4,32,2,128]{3,1,2,0:T(8,128)S(1)} all-gather(f32[1,32,2,128]{3,1,2,0:T(8,128)S(1)} %copy.17), channel_id=1, replica_groups=mesh['grp'=4,'gx'=2,'gy'=4] {'grp'}, dimensions={0}, use_global_device_ids=true | all-gather | bytes 163840 | tf_op jit(solution)/shard_map/all_gather | solution.py:222
  15.5 2.0 %collective-permute-start.24 = (f32[4,32,1,128]{3,1,2,0:T(8,128)S(1)}, f32[4,32,1,128]{3,1,2,0:T(8,128)S(1)}, u32[]{:S(2)}, u32[]{:S(2)}) collective-permute-start(f32[4,32,1,128]{3,1,2,0:T(8,128)S(1)} %get-tuple-element.39), channel_id=1, source_target_pairs={{0,4},{4,0},{1,5},{5,1},{2,6},{6,2},{3,7},{7,3},{8,12},{12,8},{9,1... | collective-permute-start | bytes 196616 | tf_op jit(solution)/shard_map/ppermute | solution.py:23
  17.6 2.5 %collective-permute-done.24 = f32[4,32,1,128]{3,1,2,0:T(8,128)S(1)} collective-permute-done((f32[4,32,1,128]{3,1,2,0:T(8,128)S(1)}, f32[4,32,1,128]{3,1,2,0:T(8,128)S(1)}, u32[]{:S(2)}, u32[]{:S(2)}) %collective-permute-start.24) | collective-permute-done | bytes 65568 | tf_op jit(solution)/shard_map/ppermute | solution.py:23
  20.1 1.6 collective-permute-done.25
  21.9 1.6 collective-permute-start.26
  23.5 2.2 %collective-permute-start.27 = (f32[4,32,4,1]{3,1,2,0:T(8,128)S(1)}, f32[4,32,4,1]{3,1,2,0:T(8,128)S(1)}, u32[]{:S(2)}, u32[]{:S(2)}) collective-permute-start(f32[4,32,4,1]{3,1,2,0:T(8,128)S(1)} %get-tuple-element.14), channel_id=1, source_target_pairs={{1,0},{2,1},{3,2},{0,3},{5,4},{6,5},{7,6},{4,7},{9,8},{10,9},{11,1... | collective-permute-start | bytes 6152 | tf_op jit(solution)/shard_map/ppermute | solution.py:26
  26.5 2.6 %broadcast_in_dim.51 = f32[8,2,2,2,128,2]{5,4,1,0,3,2:T(8,128)} broadcast(f32[8,2,128]{2,0,1:T(8,128)S(1)} %get-tuple-element.25), dimensions={0,2,4} | broadcast | bytes 73728 | tf_op jit(solution)/shard_map/broadcast_in_dim | solution.py:92
  29.0 4.0 %reshape.134 = f32[16,4,256]{2,0,1:T(8,128)S(1)} reshape(f32[8,2,2,2,128,2]{5,4,1,0,3,2:T(8,128)} %broadcast_in_dim.51) | data formatting | bytes 131072 | tf_op jit(solution)/shard_map/reshape | solution.py:95
  33.1 2.6 %broadcast_in_dim.53 = f32[8,2,2,2,128,2]{5,4,1,0,3,2:T(8,128)} broadcast(f32[8,2,128]{2,0,1:T(8,128)S(1)} %get-tuple-element.26), dimensions={0,2,4} | broadcast | bytes 73728 | tf_op jit(solution)/shard_map/broadcast_in_dim | solution.py:92
  35.6 4.0 %reshape.135 = f32[16,4,256]{2,0,1:T(8,128)S(1)} reshape(f32[8,2,2,2,128,2]{5,4,1,0,3,2:T(8,128)} %broadcast_in_dim.53) | data formatting | bytes 131072 | tf_op jit(solution)/shard_map/reshape | solution.py:95
  39.6 2.6 %broadcast_in_dim.55 = f32[8,2,2,2,128,2]{5,4,1,0,3,2:T(8,128)} broadcast(f32[8,2,128]{2,0,1:T(8,128)S(1)} %get-tuple-element.27), dimensions={0,2,4} | broadcast | bytes 73728 | tf_op jit(solution)/shard_map/broadcast_in_dim | solution.py:92
  42.2 4.0 %reshape.136 = f32[16,4,256]{2,0,1:T(8,128)S(1)} reshape(f32[8,2,2,2,128,2]{5,4,1,0,3,2:T(8,128)} %broadcast_in_dim.55) | data formatting | bytes 131072 | tf_op jit(solution)/shard_map/reshape | solution.py:95
  49.4 1.7 collective-permute-done.28
  52.7 1.9 collective-permute-start.30
  54.8 2.9 %collective-permute-done.30 = f32[32,4,1]{2,0,1:T(8,128)S(1)} collective-permute-done((f32[32,4,1]{2,0,1:T(8,128)S(1)}, f32[32,4,1]{2,0,1:T(8,128)S(1)}, u32[]{:S(2)}, u32[]{:S(2)}) %collective-permute-start.30) | collective-permute-done | bytes 544 | tf_op jit(solution)/shard_map/ppermute | solution.py:26
  57.7 3.0 %collective-permute-done.31 = f32[32,4,1]{2,0,1:T(8,128)S(1)} collective-permute-done((f32[32,4,1]{2,0,1:T(8,128)S(1)}, f32[32,4,1]{2,0,1:T(8,128)S(1)}, u32[]{:S(2)}, u32[]{:S(2)}) %collective-permute-start.31) | collective-permute-done | bytes 544 | tf_op jit(solution)/shard_map/ppermute | solution.py:23
  65.2 1.9 %collective-permute-done = f32[3,4,256]{2,0,1:T(4,128)S(1)} collective-permute-done((f32[3,4,256]{2,0,1:T(4,128)S(1)}, f32[3,4,256]{2,0,1:T(4,128)S(1)}, u32[]{:S(2)}, u32[]{:S(2)}) %collective-permute-start) | collective-permute-done | bytes 12320 | tf_op jit(solution)/shard_map/ppermute | solution.py:23
  70.1 3.0 %collective-permute-done.2 = f32[22,3,256]{2,0,1:T(8,128)S(1)} collective-permute-done((f32[22,3,256]{2,0,1:T(8,128)S(1)}, f32[22,3,256]{2,0,1:T(8,128)S(1)}, u32[]{:S(2)}, u32[]{:S(2)}) %collective-permute-start.2) | collective-permute-done | bytes 67616 | tf_op jit(solution)/shard_map/ppermute | solution.py:23
  74.9 3.8 %collective-permute-start.5 = (f32[22,10,3]{2,0,1:T(8,128)S(1)}, f32[22,10,3]{2,0,1:T(8,128)S(1)}, u32[]{:S(2)}, u32[]{:S(2)}) collective-permute-start(f32[22,10,3]{2,0,1:T(8,128)S(1)} %get-tuple-element.20), channel_id=1, source_target_pairs={{1,0},{2,1},{3,2},{0,3},{5,4},{6,5},{7,6},{4,7},{9,8},{10,9},{11,1... | collective-permute-start | bytes 7928 | tf_op jit(solution)/shard_map/ppermute | solution.py:26
  79.7 2.8 %collective-permute-done.4 = f32[22,10,3]{2,0,1:T(8,128)S(1)} collective-permute-done((f32[22,10,3]{2,0,1:T(8,128)S(1)}, f32[22,10,3]{2,0,1:T(8,128)S(1)}, u32[]{:S(2)}, u32[]{:S(2)}) %collective-permute-start.4) | collective-permute-done | bytes 2672 | tf_op jit(solution)/shard_map/ppermute | solution.py:23
  82.5 2.4 %add_add_fusion = f32[16,4,256]{2,0,1:T(8,128)S(1)} fusion(f32[16,4,256]{2,0,1:T(8,128)} %reduce-scatter.2.cloned.1.call-done, f32[16,4,256]{2,0,1:T(8,128)S(1)} %reshape.136, f32[22,10,3]{2,0,1:T(8,128)S(1)} %collective-permute-done.5, f32[22,3,256]{2,0,1:T(8,128)S(1)} %collective-permute-done.3, f32[3,4,256]{2,0,1:T(4,128)S(1)} %collective-permute-done.1, ...), kind=kLoop, calls=%fused_computation.539 | loop fusion | flops 7192576 | bytes 1082528 | tf_op jit(solution)/shard_map/add | solution.py:201
  85.1 1.7 collective-permute-start.7
  86.8 1.6 collective-permute-done.6
  90.6 2.8 %collective-permute-start.34 = (f32[32,4,1]{2,0,1:T(8,128)S(1)}, f32[32,4,1]{2,0,1:T(8,128)S(1)}, u32[]{:S(2)}, u32[]{:S(2)}) collective-permute-start(f32[32,4,1]{2,0,1:T(8,128)S(1)} %get-tuple-element.66), channel_id=1, source_target_pairs={{1,0},{2,1},{3,2},{0,3},{5,4},{6,5},{7,6},{4,7},{9,8},{10,9},{11,1... | collective-permute-start | bytes 1544 | tf_op jit(solution)/shard_map/ppermute | solution.py:26
  94.5 3.8 %collective-permute-start.11 = (f32[22,10,3]{2,0,1:T(8,128)S(1)}, f32[22,10,3]{2,0,1:T(8,128)S(1)}, u32[]{:S(2)}, u32[]{:S(2)}) collective-permute-start(f32[22,10,3]{2,0,1:T(8,128)S(1)} %get-tuple-element.18), channel_id=1, source_target_pairs={{1,0},{2,1},{3,2},{0,3},{5,4},{6,5},{7,6},{4,7},{9,8},{10,9},{11,1... | collective-permute-start | bytes 7928 | tf_op jit(solution)/shard_map/ppermute | solution.py:26
  98.4 4.4 %collective-permute-done.10 = f32[22,10,3]{2,0,1:T(8,128)S(1)} collective-permute-done((f32[22,10,3]{2,0,1:T(8,128)S(1)}, f32[22,10,3]{2,0,1:T(8,128)S(1)}, u32[]{:S(2)}, u32[]{:S(2)}) %collective-permute-start.10) | collective-permute-done | bytes 2672 | tf_op jit(solution)/shard_map/ppermute | solution.py:23
  104.6 1.7 collective-permute-start.13
  110.0 2.6 %collective-permute-done.14 = f32[22,3,256]{2,0,1:T(8,128)S(1)} collective-permute-done((f32[22,3,256]{2,0,1:T(8,128)S(1)}, f32[22,3,256]{2,0,1:T(8,128)S(1)}, u32[]{:S(2)}, u32[]{:S(2)}) %collective-permute-start.14) | collective-permute-done | bytes 67616 | tf_op jit(solution)/shard_map/ppermute | solution.py:23
  112.5 1.6 collective-permute-done.15
  114.2 2.0 %collective-permute-start.16 = (f32[22,10,3]{2,0,1:T(8,128)S(1)}, f32[22,10,3]{2,0,1:T(8,128)S(1)}, u32[]{:S(2)}, u32[]{:S(2)}) collective-permute-start(f32[22,10,3]{2,0,1:T(8,128)S(1)} %get-tuple-element.15), channel_id=1, source_target_pairs={{0,1},{1,2},{2,3},{3,0},{4,5},{5,6},{6,7},{7,4},{8,9},{9,10},{10,1... | collective-permute-start | bytes 7928 | tf_op jit(solution)/shard_map/ppermute | solution.py:23
  116.2 1.9 %collective-permute-start.17 = (f32[22,10,3]{2,0,1:T(8,128)S(1)}, f32[22,10,3]{2,0,1:T(8,128)S(1)}, u32[]{:S(2)}, u32[]{:S(2)}) collective-permute-start(f32[22,10,3]{2,0,1:T(8,128)S(1)} %get-tuple-element.16), channel_id=1, source_target_pairs={{1,0},{2,1},{3,2},{0,3},{5,4},{6,5},{7,6},{4,7},{9,8},{10,9},{11,1... | collective-permute-start | bytes 7928 | tf_op jit(solution)/shard_map/ppermute | solution.py:26
  118.2 4.1 %collective-permute-done.16 = f32[22,10,3]{2,0,1:T(8,128)S(1)} collective-permute-done((f32[22,10,3]{2,0,1:T(8,128)S(1)}, f32[22,10,3]{2,0,1:T(8,128)S(1)}, u32[]{:S(2)}, u32[]{:S(2)}) %collective-permute-start.16) | collective-permute-done | bytes 2672 | tf_op jit(solution)/shard_map/ppermute | solution.py:23
  122.3 1.6 collective-permute-done.17
  125.2 1.7 collective-permute-start.19
  131.9 1.8 collective-permute-done.20
  135.3 3.2 %collective-permute-start.23 = (f32[20,8,2]{2,0,1:T(8,128)S(1)}, f32[20,8,2]{2,0,1:T(8,128)S(1)}, u32[]{:S(2)}, u32[]{:S(2)}) collective-permute-start(f32[20,8,2]{2,0,1:T(8,128)S(1)} %get-tuple-element.24), channel_id=1, source_target_pairs={{1,0},{2,1},{3,2},{0,3},{5,4},{6,5},{7,6},{4,7},{9,8},{10,9},{11,1... | collective-permute-start | bytes 3848 | tf_op jit(solution)/shard_map/ppermute | solution.py:26
  138.9 1.7 collective-permute-start.39
  140.7 5.5 %reshape.140 = f32[8,2,2,2,128,2]{5,4,1,0,3,2:T(8,128)} reshape(f32[16,4,256]{2,0,1:T(8,128)S(1)} %get-tuple-element.9) | data formatting | bytes 131072 | tf_op jit(solution)/shard_map/reshape | solution.py:100
  146.2 2.5 %reduce_sum.39 = f32[8,2,128]{2,0,1:T(8,128)S(1)} reduce(f32[8,2,2,2,128,2]{5,4,1,0,3,2:T(8,128)} %reshape.140, f32[]{:T(128)} %constant.246.clone.1), dimensions={1,3,5}, to_apply=%region_4.5 | reduce | flops 14336 | bytes 73732 | tf_op jit(solution)/shard_map/reduce_sum | solution.py:101
  150.0 5.6 %reshape.138 = f32[8,2,2,2,128,2]{5,4,1,0,3,2:T(8,128)} reshape(f32[16,4,256]{2,0,1:T(8,128)S(1)} %get-tuple-element.54) | data formatting | bytes 131072 | tf_op jit(solution)/shard_map/reshape | solution.py:100
  155.5 2.5 %reduce_sum.37 = f32[8,2,128]{2,0,1:T(8,128)S(1)} reduce(f32[8,2,2,2,128,2]{5,4,1,0,3,2:T(8,128)} %reshape.138, f32[]{:T(128)} %constant.246.clone.1), dimensions={1,3,5}, to_apply=%region_2.3 | reduce | flops 14336 | bytes 73732 | tf_op jit(solution)/shard_map/reduce_sum | solution.py:101
  158.1 5.6 %reshape.137 = f32[8,2,2,2,128,2]{5,4,1,0,3,2:T(8,128)} reshape(f32[16,4,256]{2,0,1:T(8,128)S(1)} %get-tuple-element.5) | data formatting | bytes 131072 | tf_op jit(solution)/shard_map/reshape | solution.py:100
  163.6 2.5 %reduce_sum.36 = f32[8,2,128]{2,0,1:T(8,128)S(1)} reduce(f32[8,2,2,2,128,2]{5,4,1,0,3,2:T(8,128)} %reshape.137, f32[]{:T(128)} %constant.246.clone.1), dimensions={1,3,5}, to_apply=%region_1.2 | reduce | flops 14336 | bytes 73732 | tf_op jit(solution)/shard_map/reduce_sum | solution.py:101
  166.2 5.6 %reshape.139 = f32[8,2,2,2,128,2]{5,4,1,0,3,2:T(8,128)} reshape(f32[16,4,256]{2,0,1:T(8,128)S(1)} %get-tuple-element.55) | data formatting | bytes 131072 | tf_op jit(solution)/shard_map/reshape | solution.py:100
  171.7 2.5 %reduce_sum.38 = f32[8,2,128]{2,0,1:T(8,128)S(1)} reduce(f32[8,2,2,2,128,2]{5,4,1,0,3,2:T(8,128)} %reshape.139, f32[]{:T(128)} %constant.246.clone.1), dimensions={1,3,5}, to_apply=%region_3.4 | reduce | flops 14336 | bytes 73732 | tf_op jit(solution)/shard_map/reduce_sum | solution.py:101
  174.9 3.3 %all-to-all-start = ((f32[4,8,2,128]{3,1,2,0:T(8,128)}), f32[4,8,2,128]{3,1,2,0:T(8,128)S(1)}, u32[]{:S(2)}, u32[]{:S(2)}) async-start(f32[4,8,2,128]{3,1,2,0:T(8,128)} %pad_maximum_fusion.94), calls=%async_computation.1 | async-start | bytes 65536 | tf_op jit(solution)/shard_map/all_to_all | solution.py:214
  178.2 3.9 %all-to-all-done = f32[4,8,2,128]{3,1,2,0:T(8,128)S(1)} async-done(((f32[4,8,2,128]{3,1,2,0:T(8,128)}), f32[4,8,2,128]{3,1,2,0:T(8,128)S(1)}, u32[]{:S(2)}, u32[]{:S(2)}) %all-to-all-start) | async-done | bytes 32800 | tf_op jit(solution)/shard_map/all_to_all | solution.py:214
  (137 shorter events, 36.5 us)
Async XLA Ops:
  6.5 56.4 %reduce-scatter.2.cloned.1.call-start = ((), (), s32[]{:S(2)}) async-start(), calls=%async_computation.2 | async-start | bytes 327680 | tf_op jit(solution)/shard_map/reduce_scatter | solution.py:189
  15.5 4.6 %collective-permute-start.24 = (f32[4,32,1,128]{3,1,2,0:T(8,128)S(1)}, f32[4,32,1,128]{3,1,2,0:T(8,128)S(1)}, u32[]{:S(2)}, u32[]{:S(2)}) collective-permute-start(f32[4,32,1,128]{3,1,2,0:T(8,128)S(1)} %get-tuple-element.39), channel_id=1, source_target_pairs={{0,4},{4,0},{1,5},{5,1},{2,6},{6,2},{3,7},{7,3},{8,12},{12,8},{9,1... | collective-permute-start | bytes 196616 | tf_op jit(solution)/shard_map/ppermute | solution.py:23
  17.5 4.3 %collective-permute-start.25 = (f32[4,32,1,128]{3,1,2,0:T(8,128)S(1)}, f32[4,32,1,128]{3,1,2,0:T(8,128)S(1)}, u32[]{:S(2)}, u32[]{:S(2)}) collective-permute-start(f32[4,32,1,128]{3,1,2,0:T(8,128)S(1)} %get-tuple-element.38), channel_id=1, source_target_pairs={{4,0},{0,4},{5,1},{1,5},{6,2},{2,6},{7,3},{3,7},{12,8},{8,12},{13,... | collective-permute-start | bytes 196616 | tf_op jit(solution)/shard_map/ppermute | solution.py:26
  21.9 24.6 %collective-permute-start.26 = (f32[4,32,4,1]{3,1,2,0:T(8,128)S(1)}, f32[4,32,4,1]{3,1,2,0:T(8,128)S(1)}, u32[]{:S(2)}, u32[]{:S(2)}) collective-permute-start(f32[4,32,4,1]{3,1,2,0:T(8,128)S(1)} %get-tuple-element.13), channel_id=1, source_target_pairs={{0,1},{1,2},{2,3},{3,0},{4,5},{5,6},{6,7},{7,4},{8,9},{9,10},{10,1... | collective-permute-start | bytes 6152 | tf_op jit(solution)/shard_map/ppermute | solution.py:23
  23.5 22.9 %collective-permute-start.27 = (f32[4,32,4,1]{3,1,2,0:T(8,128)S(1)}, f32[4,32,4,1]{3,1,2,0:T(8,128)S(1)}, u32[]{:S(2)}, u32[]{:S(2)}) collective-permute-start(f32[4,32,4,1]{3,1,2,0:T(8,128)S(1)} %get-tuple-element.14), channel_id=1, source_target_pairs={{1,0},{2,1},{3,2},{0,3},{5,4},{6,5},{7,6},{4,7},{9,8},{10,9},{11,1... | collective-permute-start | bytes 6152 | tf_op jit(solution)/shard_map/ppermute | solution.py:26
  47.3 3.8 %collective-permute-start.28 = (f32[32,1,128]{2,0,1:T(8,128)S(1)}, f32[32,1,128]{2,0,1:T(8,128)S(1)}, u32[]{:S(2)}, u32[]{:S(2)}) collective-permute-start(f32[32,1,128]{2,0,1:T(8,128)S(1)} %get-tuple-element.87), channel_id=1, source_target_pairs={{4,0},{0,4},{5,1},{1,5},{6,2},{2,6},{7,3},{3,7},{12,8},{8,12},{13,... | collective-permute-start | bytes 49160 | tf_op jit(solution)/shard_map/ppermute | solution.py:26
  48.9 3.7 %collective-permute-start.29 = (f32[32,1,128]{2,0,1:T(8,128)S(1)}, f32[32,1,128]{2,0,1:T(8,128)S(1)}, u32[]{:S(2)}, u32[]{:S(2)}) collective-permute-start(f32[32,1,128]{2,0,1:T(8,128)S(1)} %get-tuple-element.86), channel_id=1, source_target_pairs={{0,4},{4,0},{1,5},{5,1},{2,6},{6,2},{3,7},{7,3},{8,12},{12,8},{9,1... | collective-permute-start | bytes 49160 | tf_op jit(solution)/shard_map/ppermute | solution.py:23
  52.7 4.9 %collective-permute-start.30 = (f32[32,4,1]{2,0,1:T(8,128)S(1)}, f32[32,4,1]{2,0,1:T(8,128)S(1)}, u32[]{:S(2)}, u32[]{:S(2)}) collective-permute-start(f32[32,4,1]{2,0,1:T(8,128)S(1)} %get-tuple-element.68), channel_id=1, source_target_pairs={{1,0},{2,1},{3,2},{0,3},{5,4},{6,5},{7,6},{4,7},{9,8},{10,9},{11,1... | collective-permute-start | bytes 1544 | tf_op jit(solution)/shard_map/ppermute | solution.py:26
  54.6 6.1 %collective-permute-start.31 = (f32[32,4,1]{2,0,1:T(8,128)S(1)}, f32[32,4,1]{2,0,1:T(8,128)S(1)}, u32[]{:S(2)}, u32[]{:S(2)}) collective-permute-start(f32[32,4,1]{2,0,1:T(8,128)S(1)} %get-tuple-element.69), channel_id=1, source_target_pairs={{0,1},{1,2},{2,3},{3,0},{4,5},{5,6},{6,7},{7,4},{8,9},{9,10},{10,1... | collective-permute-start | bytes 1544 | tf_op jit(solution)/shard_map/ppermute | solution.py:23
  60.8 26.0 %collective-permute-start.32 = (f32[32,1,128]{2,0,1:T(8,128)S(1)}, f32[32,1,128]{2,0,1:T(8,128)S(1)}, u32[]{:S(2)}, u32[]{:S(2)}) collective-permute-start(f32[32,1,128]{2,0,1:T(8,128)S(1)} %get-tuple-element.81), channel_id=1, source_target_pairs={{4,0},{0,4},{5,1},{1,5},{6,2},{2,6},{7,3},{3,7},{12,8},{8,12},{13,... | collective-permute-start | bytes 49160 | tf_op jit(solution)/shard_map/ppermute | solution.py:26
  61.4 25.4 %collective-permute-start.33 = (f32[32,1,128]{2,0,1:T(8,128)S(1)}, f32[32,1,128]{2,0,1:T(8,128)S(1)}, u32[]{:S(2)}, u32[]{:S(2)}) collective-permute-start(f32[32,1,128]{2,0,1:T(8,128)S(1)} %get-tuple-element.80), channel_id=1, source_target_pairs={{0,4},{4,0},{1,5},{5,1},{2,6},{6,2},{3,7},{7,3},{8,12},{12,8},{9,1... | collective-permute-start | bytes 49160 | tf_op jit(solution)/shard_map/ppermute | solution.py:23
  62.9 40.6 %copy-start = (f32[16,4,256]{2,0,1:T(8,128)S(1)}, f32[16,4,256]{2,0,1:T(8,128)}, u32[]{:S(2)}) copy-start(f32[16,4,256]{2,0,1:T(8,128)} %reduce-scatter.2.cloned.1.call-done) | copy-start | bytes 196612
  63.7 1.4 collective-permute-start.1
  63.7 3.4 %collective-permute-start = (f32[3,4,256]{2,0,1:T(4,128)S(1)}, f32[3,4,256]{2,0,1:T(4,128)S(1)}, u32[]{:S(2)}, u32[]{:S(2)}) collective-permute-start(f32[3,4,256]{2,0,1:T(4,128)S(1)} %get-tuple-element.62), channel_id=1, source_target_pairs={{0,8},{8,16},{16,24},{24,0},{1,9},{9,17},{17,25},{25,1},{2,10},{10... | collective-permute-start | bytes 36872 | tf_op jit(solution)/shard_map/ppermute | solution.py:23
  68.0 5.1 %collective-permute-start.2 = (f32[22,3,256]{2,0,1:T(8,128)S(1)}, f32[22,3,256]{2,0,1:T(8,128)S(1)}, u32[]{:S(2)}, u32[]{:S(2)}) collective-permute-start(f32[22,3,256]{2,0,1:T(8,128)S(1)} %get-tuple-element.52), channel_id=1, source_target_pairs={{0,4},{4,0},{1,5},{5,1},{2,6},{6,2},{3,7},{7,3},{8,12},{12,8},{9,1... | collective-permute-start | bytes 202760 | tf_op jit(solution)/shard_map/ppermute | solution.py:23
  68.6 5.3 %collective-permute-start.3 = (f32[22,3,256]{2,0,1:T(8,128)S(1)}, f32[22,3,256]{2,0,1:T(8,128)S(1)}, u32[]{:S(2)}, u32[]{:S(2)}) collective-permute-start(f32[22,3,256]{2,0,1:T(8,128)S(1)} %get-tuple-element.53), channel_id=1, source_target_pairs={{4,0},{0,4},{5,1},{1,5},{6,2},{2,6},{7,3},{3,7},{12,8},{8,12},{13,... | collective-permute-start | bytes 202760 | tf_op jit(solution)/shard_map/ppermute | solution.py:26
  74.9 7.6 %collective-permute-start.4 = (f32[22,10,3]{2,0,1:T(8,128)S(1)}, f32[22,10,3]{2,0,1:T(8,128)S(1)}, u32[]{:S(2)}, u32[]{:S(2)}) collective-permute-start(f32[22,10,3]{2,0,1:T(8,128)S(1)} %get-tuple-element.19), channel_id=1, source_target_pairs={{0,1},{1,2},{2,3},{3,0},{4,5},{5,6},{6,7},{7,4},{8,9},{9,10},{10,1... | collective-permute-start | bytes 7928 | tf_op jit(solution)/shard_map/ppermute | solution.py:23
  74.9 7.6 %collective-permute-start.5 = (f32[22,10,3]{2,0,1:T(8,128)S(1)}, f32[22,10,3]{2,0,1:T(8,128)S(1)}, u32[]{:S(2)}, u32[]{:S(2)}) collective-permute-start(f32[22,10,3]{2,0,1:T(8,128)S(1)} %get-tuple-element.20), channel_id=1, source_target_pairs={{1,0},{2,1},{3,2},{0,3},{5,4},{6,5},{7,6},{4,7},{9,8},{10,9},{11,1... | collective-permute-start | bytes 7928 | tf_op jit(solution)/shard_map/ppermute | solution.py:26
  85.0 40.1 %copy-start.1 = (s32[4,256]{1,0:T(4,128)S(1)}, s32[4,256]{1,0:T(4,128)}, u32[]{:S(2)}) copy-start(s32[4,256]{1,0:T(4,128)} %param.7) | copy-start | bytes 12292
  85.0 3.4 %collective-permute-start.6 = (f32[3,4,256]{2,0,1:T(4,128)S(1)}, f32[3,4,256]{2,0,1:T(4,128)S(1)}, u32[]{:S(2)}, u32[]{:S(2)}) collective-permute-start(f32[3,4,256]{2,0,1:T(4,128)S(1)} %get-tuple-element.60), channel_id=1, source_target_pairs={{0,8},{8,16},{16,24},{24,0},{1,9},{9,17},{17,25},{25,1},{2,10},{10... | collective-permute-start | bytes 36872 | tf_op jit(solution)/shard_map/ppermute | solution.py:23
  85.1 3.3 %collective-permute-start.7 = (f32[3,4,256]{2,0,1:T(4,128)S(1)}, f32[3,4,256]{2,0,1:T(4,128)S(1)}, u32[]{:S(2)}, u32[]{:S(2)}) collective-permute-start(f32[3,4,256]{2,0,1:T(4,128)S(1)} %get-tuple-element.61), channel_id=1, source_target_pairs={{8,0},{16,8},{24,16},{0,24},{9,1},{17,9},{25,17},{1,25},{10,2},{18... | collective-permute-start | bytes 36872 | tf_op jit(solution)/shard_map/ppermute | solution.py:26
  88.4 5.1 %collective-permute-start.8 = (f32[22,3,256]{2,0,1:T(8,128)S(1)}, f32[22,3,256]{2,0,1:T(8,128)S(1)}, u32[]{:S(2)}, u32[]{:S(2)}) collective-permute-start(f32[22,3,256]{2,0,1:T(8,128)S(1)} %get-tuple-element.48), channel_id=1, source_target_pairs={{0,4},{4,0},{1,5},{5,1},{2,6},{6,2},{3,7},{7,3},{8,12},{12,8},{9,1... | collective-permute-start | bytes 202760 | tf_op jit(solution)/shard_map/ppermute | solution.py:23
  89.1 5.2 %collective-permute-start.9 = (f32[22,3,256]{2,0,1:T(8,128)S(1)}, f32[22,3,256]{2,0,1:T(8,128)S(1)}, u32[]{:S(2)}, u32[]{:S(2)}) collective-permute-start(f32[22,3,256]{2,0,1:T(8,128)S(1)} %get-tuple-element.49), channel_id=1, source_target_pairs={{4,0},{0,4},{5,1},{1,5},{6,2},{2,6},{7,3},{3,7},{12,8},{8,12},{13,... | collective-permute-start | bytes 202760 | tf_op jit(solution)/shard_map/ppermute | solution.py:26
  90.6 15.8 %collective-permute-start.34 = (f32[32,4,1]{2,0,1:T(8,128)S(1)}, f32[32,4,1]{2,0,1:T(8,128)S(1)}, u32[]{:S(2)}, u32[]{:S(2)}) collective-permute-start(f32[32,4,1]{2,0,1:T(8,128)S(1)} %get-tuple-element.66), channel_id=1, source_target_pairs={{1,0},{2,1},{3,2},{0,3},{5,4},{6,5},{7,6},{4,7},{9,8},{10,9},{11,1... | collective-permute-start | bytes 1544 | tf_op jit(solution)/shard_map/ppermute | solution.py:26
  93.4 13.0 %collective-permute-start.35 = (f32[32,4,1]{2,0,1:T(8,128)S(1)}, f32[32,4,1]{2,0,1:T(8,128)S(1)}, u32[]{:S(2)}, u32[]{:S(2)}) collective-permute-start(f32[32,4,1]{2,0,1:T(8,128)S(1)} %get-tuple-element.67), channel_id=1, source_target_pairs={{0,1},{1,2},{2,3},{3,0},{4,5},{5,6},{6,7},{7,4},{8,9},{9,10},{10,1... | collective-permute-start | bytes 1544 | tf_op jit(solution)/shard_map/ppermute | solution.py:23
  94.5 8.4 %collective-permute-start.10 = (f32[22,10,3]{2,0,1:T(8,128)S(1)}, f32[22,10,3]{2,0,1:T(8,128)S(1)}, u32[]{:S(2)}, u32[]{:S(2)}) collective-permute-start(f32[22,10,3]{2,0,1:T(8,128)S(1)} %get-tuple-element.17), channel_id=1, source_target_pairs={{0,1},{1,2},{2,3},{3,0},{4,5},{5,6},{6,7},{7,4},{8,9},{9,10},{10,1... | collective-permute-start | bytes 7928 | tf_op jit(solution)/shard_map/ppermute | solution.py:23
  94.5 8.9 %collective-permute-start.11 = (f32[22,10,3]{2,0,1:T(8,128)S(1)}, f32[22,10,3]{2,0,1:T(8,128)S(1)}, u32[]{:S(2)}, u32[]{:S(2)}) collective-permute-start(f32[22,10,3]{2,0,1:T(8,128)S(1)} %get-tuple-element.18), channel_id=1, source_target_pairs={{1,0},{2,1},{3,2},{0,3},{5,4},{6,5},{7,6},{4,7},{9,8},{10,9},{11,1... | collective-permute-start | bytes 7928 | tf_op jit(solution)/shard_map/ppermute | solution.py:26
  104.6 3.2 %collective-permute-start.12 = (f32[3,4,256]{2,0,1:T(4,128)S(1)}, f32[3,4,256]{2,0,1:T(4,128)S(1)}, u32[]{:S(2)}, u32[]{:S(2)}) collective-permute-start(f32[3,4,256]{2,0,1:T(4,128)S(1)} %get-tuple-element.58), channel_id=1, source_target_pairs={{0,8},{8,16},{16,24},{24,0},{1,9},{9,17},{17,25},{25,1},{2,10},{10... | collective-permute-start | bytes 36872 | tf_op jit(solution)/shard_map/ppermute | solution.py:23
  104.6 3.2 %collective-permute-start.13 = (f32[3,4,256]{2,0,1:T(4,128)S(1)}, f32[3,4,256]{2,0,1:T(4,128)S(1)}, u32[]{:S(2)}, u32[]{:S(2)}) collective-permute-start(f32[3,4,256]{2,0,1:T(4,128)S(1)} %get-tuple-element.59), channel_id=1, source_target_pairs={{8,0},{16,8},{24,16},{0,24},{9,1},{17,9},{25,17},{1,25},{10,2},{18... | collective-permute-start | bytes 36872 | tf_op jit(solution)/shard_map/ppermute | solution.py:26
  107.9 4.7 %collective-permute-start.14 = (f32[22,3,256]{2,0,1:T(8,128)S(1)}, f32[22,3,256]{2,0,1:T(8,128)S(1)}, u32[]{:S(2)}, u32[]{:S(2)}) collective-permute-start(f32[22,3,256]{2,0,1:T(8,128)S(1)} %get-tuple-element.44), channel_id=1, source_target_pairs={{0,4},{4,0},{1,5},{5,1},{2,6},{6,2},{3,7},{7,3},{8,12},{12,8},{9,1... | collective-permute-start | bytes 202760 | tf_op jit(solution)/shard_map/ppermute | solution.py:23
  108.9 5.2 %collective-permute-start.15 = (f32[22,3,256]{2,0,1:T(8,128)S(1)}, f32[22,3,256]{2,0,1:T(8,128)S(1)}, u32[]{:S(2)}, u32[]{:S(2)}) collective-permute-start(f32[22,3,256]{2,0,1:T(8,128)S(1)} %get-tuple-element.45), channel_id=1, source_target_pairs={{4,0},{0,4},{5,1},{1,5},{6,2},{2,6},{7,3},{3,7},{12,8},{8,12},{13,... | collective-permute-start | bytes 202760 | tf_op jit(solution)/shard_map/ppermute | solution.py:26
  114.2 8.0 %collective-permute-start.16 = (f32[22,10,3]{2,0,1:T(8,128)S(1)}, f32[22,10,3]{2,0,1:T(8,128)S(1)}, u32[]{:S(2)}, u32[]{:S(2)}) collective-permute-start(f32[22,10,3]{2,0,1:T(8,128)S(1)} %get-tuple-element.15), channel_id=1, source_target_pairs={{0,1},{1,2},{2,3},{3,0},{4,5},{5,6},{6,7},{7,4},{8,9},{9,10},{10,1... | collective-permute-start | bytes 7928 | tf_op jit(solution)/shard_map/ppermute | solution.py:23
  116.2 7.7 %collective-permute-start.17 = (f32[22,10,3]{2,0,1:T(8,128)S(1)}, f32[22,10,3]{2,0,1:T(8,128)S(1)}, u32[]{:S(2)}, u32[]{:S(2)}) collective-permute-start(f32[22,10,3]{2,0,1:T(8,128)S(1)} %get-tuple-element.16), channel_id=1, source_target_pairs={{1,0},{2,1},{3,2},{0,3},{5,4},{6,5},{7,6},{4,7},{9,8},{10,9},{11,1... | collective-permute-start | bytes 7928 | tf_op jit(solution)/shard_map/ppermute | solution.py:26
  125.1 3.8 %collective-permute-start.18 = (f32[2,4,256]{2,0,1:T(2,128)S(1)}, f32[2,4,256]{2,0,1:T(2,128)S(1)}, u32[]{:S(2)}, u32[]{:S(2)}) collective-permute-start(f32[2,4,256]{2,0,1:T(2,128)S(1)} %get-tuple-element.56), channel_id=1, source_target_pairs={{0,8},{8,16},{16,24},{24,0},{1,9},{9,17},{17,25},{25,1},{2,10},{10... | collective-permute-start | bytes 24584 | tf_op jit(solution)/shard_map/ppermute | solution.py:23
  125.2 3.8 %collective-permute-start.19 = (f32[2,4,256]{2,0,1:T(2,128)S(1)}, f32[2,4,256]{2,0,1:T(2,128)S(1)}, u32[]{:S(2)}, u32[]{:S(2)}) collective-permute-start(f32[2,4,256]{2,0,1:T(2,128)S(1)} %get-tuple-element.57), channel_id=1, source_target_pairs={{8,0},{16,8},{24,16},{0,24},{9,1},{17,9},{25,17},{1,25},{10,2},{18... | collective-permute-start | bytes 24584 | tf_op jit(solution)/shard_map/ppermute | solution.py:26
  126.9 4.2 %collective-permute-start.36 = (f32[32,1,128]{2,0,1:T(8,128)S(1)}, f32[32,1,128]{2,0,1:T(8,128)S(1)}, u32[]{:S(2)}, u32[]{:S(2)}) collective-permute-start(f32[32,1,128]{2,0,1:T(8,128)S(1)} %get-tuple-element.75), channel_id=1, source_target_pairs={{4,0},{0,4},{5,1},{1,5},{6,2},{2,6},{7,3},{3,7},{12,8},{8,12},{13,... | collective-permute-start | bytes 49160 | tf_op jit(solution)/shard_map/ppermute | solution.py:26
  128.1 3.7 %collective-permute-start.37 = (f32[32,1,128]{2,0,1:T(8,128)S(1)}, f32[32,1,128]{2,0,1:T(8,128)S(1)}, u32[]{:S(2)}, u32[]{:S(2)}) collective-permute-start(f32[32,1,128]{2,0,1:T(8,128)S(1)} %get-tuple-element.74), channel_id=1, source_target_pairs={{0,4},{4,0},{1,5},{5,1},{2,6},{6,2},{3,7},{7,3},{8,12},{12,8},{9,1... | collective-permute-start | bytes 49160 | tf_op jit(solution)/shard_map/ppermute | solution.py:23
  129.0 4.7 %collective-permute-start.20 = (f32[20,2,256]{2,0,1:T(8,128)S(1)}, f32[20,2,256]{2,0,1:T(8,128)S(1)}, u32[]{:S(2)}, u32[]{:S(2)}) collective-permute-start(f32[20,2,256]{2,0,1:T(8,128)S(1)} %get-tuple-element.40), channel_id=1, source_target_pairs={{0,4},{4,0},{1,5},{5,1},{2,6},{6,2},{3,7},{7,3},{8,12},{12,8},{9,1... | collective-permute-start | bytes 122888 | tf_op jit(solution)/shard_map/ppermute | solution.py:23
  130.3 4.3 %collective-permute-start.21 = (f32[20,2,256]{2,0,1:T(8,128)S(1)}, f32[20,2,256]{2,0,1:T(8,128)S(1)}, u32[]{:S(2)}, u32[]{:S(2)}) collective-permute-start(f32[20,2,256]{2,0,1:T(8,128)S(1)} %get-tuple-element.41), channel_id=1, source_target_pairs={{4,0},{0,4},{5,1},{1,5},{6,2},{2,6},{7,3},{3,7},{12,8},{8,12},{13,... | collective-permute-start | bytes 122888 | tf_op jit(solution)/shard_map/ppermute | solution.py:26
  134.7 14.1 %collective-permute-start.22 = (f32[20,8,2]{2,0,1:T(8,128)S(1)}, f32[20,8,2]{2,0,1:T(8,128)S(1)}, u32[]{:S(2)}, u32[]{:S(2)}) collective-permute-start(f32[20,8,2]{2,0,1:T(8,128)S(1)} %get-tuple-element.23), channel_id=1, source_target_pairs={{0,1},{1,2},{2,3},{3,0},{4,5},{5,6},{6,7},{7,4},{8,9},{9,10},{10,1... | collective-permute-start | bytes 3848 | tf_op jit(solution)/shard_map/ppermute | solution.py:23
  135.3 13.5 %collective-permute-start.23 = (f32[20,8,2]{2,0,1:T(8,128)S(1)}, f32[20,8,2]{2,0,1:T(8,128)S(1)}, u32[]{:S(2)}, u32[]{:S(2)}) collective-permute-start(f32[20,8,2]{2,0,1:T(8,128)S(1)} %get-tuple-element.24), channel_id=1, source_target_pairs={{1,0},{2,1},{3,2},{0,3},{5,4},{6,5},{7,6},{4,7},{9,8},{10,9},{11,1... | collective-permute-start | bytes 3848 | tf_op jit(solution)/shard_map/ppermute | solution.py:26
  138.6 39.6 %collective-permute-start.38 = (f32[32,4,1]{2,0,1:T(8,128)S(1)}, f32[32,4,1]{2,0,1:T(8,128)S(1)}, u32[]{:S(2)}, u32[]{:S(2)}) collective-permute-start(f32[32,4,1]{2,0,1:T(8,128)S(1)} %get-tuple-element.64), channel_id=1, source_target_pairs={{1,0},{2,1},{3,2},{0,3},{5,4},{6,5},{7,6},{4,7},{9,8},{10,9},{11,1... | collective-permute-start | bytes 1544 | tf_op jit(solution)/shard_map/ppermute | solution.py:26
  138.9 39.3 %collective-permute-start.39 = (f32[32,4,1]{2,0,1:T(8,128)S(1)}, f32[32,4,1]{2,0,1:T(8,128)S(1)}, u32[]{:S(2)}, u32[]{:S(2)}) collective-permute-start(f32[32,4,1]{2,0,1:T(8,128)S(1)} %get-tuple-element.65), channel_id=1, source_target_pairs={{0,1},{1,2},{2,3},{3,0},{4,5},{5,6},{6,7},{7,4},{8,9},{9,10},{10,1... | collective-permute-start | bytes 1544 | tf_op jit(solution)/shard_map/ppermute | solution.py:23
  174.9 7.2 %all-to-all-start = ((f32[4,8,2,128]{3,1,2,0:T(8,128)}), f32[4,8,2,128]{3,1,2,0:T(8,128)S(1)}, u32[]{:S(2)}, u32[]{:S(2)}) async-start(f32[4,8,2,128]{3,1,2,0:T(8,128)} %pad_maximum_fusion.94), calls=%async_computation.1 | async-start | bytes 65536 | tf_op jit(solution)/shard_map/all_to_all | solution.py:214
Sparse Core Ops, SparseCore 0:
  9.8 22.7 reduce-scatter.1
where the time goes:
time: 190 us
  starting transfers between devices  52.1 us (27%)
  waiting for transfers between devices  48.1 us (25%)
  local copies, waits for them, and re-layouts  46.5 us (24%)
  other arithmetic  22.7 us (12%)
  between operations  13.9 us (7%)
  blocking collectives  6.47 us (3%)
    ppermute x20, starting transfers between devices, extended(): lax.ppermute(lax.slice_in_dim(block, 0, width, axis=dim), axis, backward)  33.4 us
    ppermute x20, waiting for transfers between devices, extended(): lax.ppermute(lax.slice_in_dim(block, block.shape[dim] - width, None, axis...  31.5 us
    reshape x4, local copies, waits for them, and re-layouts, coarsen(): fine_field.reshape(plane_count // 2, 2, height // 2, 2, breadth // 2, 2)  22.2 us
    ppermute x20, starting transfers between devices, extended(): lax.ppermute(lax.slice_in_dim(block, block.shape[dim] - width, None, axis...  15.4 us
    ppermute x20, waiting for transfers between devices, extended(): lax.ppermute(lax.slice_in_dim(block, 0, width, axis=dim), axis, backward)  12.7 us
    reshape x3, local copies, waits for them, and re-layouts, refine(): return spread_out.reshape(2 * plane_count, 2 * height, 2 * breadth)  12.1 us
    reduce_sum x4, other arithmetic, coarsen(): return jnp.sum(blocks, axis=(1, 3, 5)) * 0.125  10.2 us
    broadcast_in_dim x4, local copies, waits for them, and re-layouts, refine(): jnp.broadcast_to(coarse[:, None, :, None, :, None], (plane_count, 2, heig...  7.66 us
  transfers between devices with their start and end apart: 42, of which 25 were waited for; matrix products, arithmetic and copies ran while one was open for 34% of the time, Pallas kernels for 0%

commit v1 on v0

--- a/solution.py
+++ b/solution.py
@@ -1,6 +1,10 @@
+import functools
+
 import jax
 import jax.numpy as jnp
 from jax import lax
+from jax.experimental import pallas as pl
+from jax.experimental.pallas import tpu as pltpu
 from jax.sharding import PartitionSpec as P
 
 SWEEPS = 3
@@ -215,7 +219,7 @@
     return (received, received[0])
 
 
-def on_device(flow_fields, level_set, band_tiles, nozzle_phase):
+def on_device_general(flow_fields, level_set, band_tiles, nozzle_phase):
     group = lax.axis_index("grp")
     component = jnp.minimum(group, 2)
     is_level = group == 3
@@ -236,6 +240,513 @@
     return result[None]
 
 
+MESH = pl.DeviceIdType.MESH
+LANES = 128
+ROWS = 8
+EXACT = lax.Precision.HIGHEST
+
+
+def lanes_of(shape, dim=1):
+    return lax.broadcasted_iota(jnp.int32, shape, dim)
+
+
+def along_z(block, offset, period):
+    spot = lanes_of(block.shape) % period
+    plain = pltpu.roll(block, (-offset) % LANES, 1)
+    if offset > 0:
+        around = pltpu.roll(block, (period - offset) % LANES, 1)
+        return jnp.where(spot < period - offset, plain, around)
+    around = pltpu.roll(block, (-period - offset) % LANES, 1)
+    return jnp.where(spot >= -offset, plain, around)
+
+
+def along_rows(block, offset):
+    return pltpu.roll(block, (-offset) % block.shape[0], 0)
+
+
+def weno_upwind(diffs, speed):
+    forward = speed >= 0.0
+    one = jnp.where(forward, diffs[0], diffs[5])
+    two = jnp.where(forward, diffs[1], diffs[4])
+    three = jnp.where(forward, diffs[2], diffs[3])
+    four = jnp.where(forward, diffs[3], diffs[2])
+    five = jnp.where(forward, diffs[4], diffs[1])
+    step_a = two - one
+    step_b = three - two
+    step_c = four - three
+    step_d = five - four
+
+    def weight(curve, slope):
+        rough = (WENO_EPS * 12.0 / 13.0) + curve * curve + (3.0 / 13.0) * (slope * slope)
+        inverse = 1.0 / rough
+        return inverse * inverse
+
+    weight_one = weight(step_b - step_a, 3.0 * step_b - step_a)
+    weight_two = 6.0 * weight(step_c - step_b, step_c + step_b)
+    weight_three = 3.0 * weight(step_d - step_c, 3.0 * step_c - step_d)
+    mixed = (
+        weight_one * (5.0 * step_b - 2.0 * step_a)
+        + weight_two * (step_b + 2.0 * step_c)
+        + weight_three * (4.0 * step_c - step_d)
+    )
+    total = weight_one + weight_two + weight_three
+    return three + mixed / (6.0 * total)
+
+
+def window(index, count, chunk, margin):
+    low = index * chunk - margin
+    high = (index + 1) * chunk + margin
+    start, stop = max(low, 0), min(high, count * chunk)
+    return start, stop - start, start - low
+
+
+def brick_kernel(
+    plan,
+    flow_ref,
+    level_ref,
+    marks_ref,
+    out_ref,
+    flow_turned,
+    level_turned,
+    marks_turned,
+    flow_in,
+    level_in,
+    marks_in,
+    speeds,
+    stage_one,
+    stage_two,
+    shaped,
+    normals,
+    packed,
+    results,
+    gathered,
+    send_sems,
+    take_sems,
+):
+    groups, halves, rings = plan["groups"], plan["halves"], plan["rings"]
+    chunks = groups * halves
+    fine_chunk, flow_chunk = plan["fine_chunk"], plan["flow_chunk"]
+    fine_z, flow_z = plan["fine_z"], plan["flow_z"]
+    fine_margin, mark_margin, flow_margin = 2 * ROWS, ROWS, ROWS
+    pairs = level_ref.shape[0]
+    majors = pairs * halves
+    group = lax.axis_index("grp")
+    half = lax.axis_index("gx")
+    ring = lax.axis_index("gy")
+    after = lax.rem(ring + 1, rings)
+    before = lax.rem(ring + rings - 1, rings)
+    mine = group * halves + half
+    last = chunks - 1
+
+    barrier = pltpu.get_barrier_semaphore()
+
+    def greet(target_group, target_half, target_ring):
+        pl.semaphore_signal(
+            barrier,
+            inc=1,
+            device_id=(target_group, target_half, target_ring),
+            device_id_type=MESH,
+        )
+
+    for chunk in range(chunks):
+        tg, th = chunk // halves, chunk % halves
+
+        @pl.when(mine != chunk)
+        def _(tg=tg, th=th):
+            greet(tg, th, ring)
+
+        @pl.when(mine == 0)
+        def _(tg=tg, th=th):
+            greet(tg, th, before)
+
+        @pl.when(mine == last)
+        def _(tg=tg, th=th):
+            greet(tg, th, after)
+
+    @pl.when(group == groups - 1)
+    def _():
+        for pair in range(pairs):
+            level_turned[pair] = level_ref[pair].T
+
+    doubled = jnp.concatenate([flow_ref[...]] * halves, axis=0)
+    flow_turned[...] = doubled.T
+    marks_turned[...] = marks_ref[...].T
+
+    pl.semaphore_wait(barrier, chunks + 1)
+
+    sent = []
+
+    def push(source, target, chunk, ring_to, take, condition=None):
+        tg, th = chunk // halves, chunk % halves
+        slot = len(sent)
+        remote = pltpu.make_async_remote_copy(
+            src_ref=source,
+            dst_ref=target,
+            send_sem=send_sems.at[slot],
+            recv_sem=take_sems.at[take],
+            device_id=(tg, th, ring_to),
+            device_id_type=MESH,
+        )
+        near = ring_to is ring
+        far = mine != chunk if near else None
+        if condition is not None:
+            far = condition if far is None else jnp.logical_and(condition, far)
+        if near:
+            here = mine == chunk
+            if condition is not None:
+                here = jnp.logical_and(condition, here)
+
+            @pl.when(here)
+            def _():
+                pltpu.make_async_copy(source, target, take_sems.at[take]).start()
+
+        if far is None:
+            remote.start()
+        else:
+            pl.when(far)(remote.start)
+        sent.append((far, remote))
+
+    holder = group == groups - 1
+    major_spot = pl.ds(half * pairs, pairs)
+    for chunk in range(chunks):
+        start, count, spot = window(chunk, chunks, fine_chunk, fine_margin)
+        push(
+            level_turned.at[:, pl.ds(start, count)],
+            level_in.at[major_spot, pl.ds(spot, count)],
+            chunk,
+            ring,
+            0,
+            holder,
+        )
+    fine_rows = chunks * fine_chunk
+    push(
+        level_turned.at[:, pl.ds(fine_rows - fine_margin, fine_margin)],
+        level_in.at[major_spot, pl.ds(0, fine_margin)],
+        0,
+        after,
+        0,
+        holder,
+    )
+    push(
+        level_turned.at[:, pl.ds(0, fine_margin)],
+        level_in.at[major_spot, pl.ds(fine_margin + fine_chunk, fine_margin)],
+        last,
+        before,
+        0,
+        holder,
+    )
+    for chunk in range(chunks):
+        start, count, spot = window(chunk, chunks, flow_chunk, flow_margin)
+        push(
+            flow_turned.at[pl.ds(start, count)],
+            flow_in.at[group, half, pl.ds(spot, count)],
+            chunk,
+            ring,
+            1,
+        )
+    flow_rows = chunks * flow_chunk
+    push(
+        flow_turned.at[pl.ds(flow_rows - flow_margin, flow_margin)],
+        flow_in.at[group, half, pl.ds(0, flow_margin)],
+        0,
+        after,
+        1,
+    )
+    push(
+        flow_turned.at[pl.ds(0, flow_margin)],
+        flow_in.at[group, half, pl.ds(flow_margin + flow_chunk, flow_margin)],
+        last,
+        before,
+        1,
+    )
+    for chunk in range(chunks):
+        start, count, spot = window(chunk, chunks, fine_chunk, mark_margin)
+        push(
+            marks_turned.at[pl.ds(start, count)],
+            marks_in.at[half, pl.ds(spot, count)],
+            chunk,
+            ring,
+            2,
+            group == chunk // halves,
+        )
+    push(
+        marks_turned.at[pl.ds(fine_rows - mark_margin, mark_margin)],
+        marks_in.at[half, pl.ds(0, mark_margin)],
+        0,
+        after,
+        2,
+        group == 0,
+    )
+    push(
+        marks_turned.at[pl.ds(0, mark_margin)],
+        marks_in.at[half, pl.ds(mark_margin + fine_chunk, mark_margin)],
+        last,
+        before,
+        2,
+        group == groups - 1,
+    )
+
+    body = fine_chunk + 2 * mark_margin
+    offset = fine_margin - mark_margin
+    edge = jnp.zeros((majors, offset, LANES), jnp.float32)
+    for stage in (stage_one, stage_two):
+        stage[:, pl.ds(0, offset)] = edge
+        stage[:, pl.ds(offset + body, offset)] = edge
+
+    pltpu.make_async_copy(flow_in, flow_in, take_sems.at[1]).wait()
+    share = LANES // halves
+    fields = []
+    flow_lane = lanes_of((flow_chunk + 2 * flow_margin, LANES))
+    for field in range(groups):
+        merged = flow_in[field, 0]
+        for part in range(1, halves):
+            merged = jnp.where(flow_lane >= part * share, flow_in[field, part], merged)
+        fields.append(merged)
+
+    from_flow = lax.broadcasted_iota(jnp.int32, (LANES, majors * LANES), 0)
+    to_fine = lanes_of((LANES, majors * LANES))
+    fine_cell = (to_fine // LANES) * flow_z + (to_fine % fine_z) // 2
+    spread_lanes = (from_flow == fine_cell).astype(jnp.float32)
+    flow_window = flow_chunk + 2 * flow_margin
+    spread_rows = (
+        lanes_of((body, flow_window))
+        == lax.broadcasted_iota(jnp.int32, (body, flow_window), 0) // 2
+        + (flow_margin - mark_margin // 2)
+    ).astype(jnp.float32)
+    for direction in range(3):
+        tall = jnp.dot(
+            spread_rows, fields[direction], precision=EXACT, preferred_element_type=jnp.float32
+        )
+        wide = jnp.dot(tall, spread_lanes, precision=EXACT, preferred_element_type=jnp.float32)
+        for major in range(majors):
+            speeds[direction, major] = wide[:, major * LANES : (major + 1) * LANES]
+
+    def flow_beside(block, direction, step):
+        if direction == 0:
+            return pltpu.roll(block, (-step * flow_z) % LANES, 1)
+        if direction == 1:
+            return along_rows(block, step)
+        return along_z(block, step, flow_z)
+
+    def flow_slope(block, direction):
+        return 0.5 * (flow_beside(block, direction, 1) - flow_beside(block, direction, -1))
+
+    moved = []
+    for component in range(3):
+        moving = fields[component]
+        advect = fields[0] * flow_slope(moving, 0)
+        advect = advect + fields[1] * flow_slope(moving, 1)
+        advect = advect + fields[2] * flow_slope(moving, 2)
+        source = moving - STEP_FLOW * (advect + flow_slope(fields[3], component))
+        relaxed = source
+        for sweep_number in range(SWEEPS):
+            beside = jnp.zeros_like(relaxed)
+            for direction in range(3):
+                beside = beside + flow_beside(relaxed, direction, 1)
+                beside = beside + flow_beside(relaxed, direction, -1)
+            relaxed = (source + IMPLICIT * beside) * (1.0 / (1.0 + 6.0 * IMPLICIT))
+        moved.append(relaxed[flow_margin : flow_margin + flow_chunk])
+
+    pltpu.make_async_copy(level_in, level_in, take_sems.at[0]).wait()
+
+    block_rows = 2 * ROWS
+
+    def section(current, target, keep, blend):
+        def one(major, carry):
+            def far_major(step):
+                return lax.rem(major + majors + step, majors)
+
+            for start in range(0, body, block_rows):
+                rows = pl.ds(offset + start, block_rows)
+                tall = current[major, pl.ds(start, block_rows + 2 * offset)]
+                middle = tall[offset : offset + block_rows]
+                low_half = lanes_of(middle.shape) < fine_z
+                whole = {step: current[far_major(step), rows] for step in (-2, -1, 1, 2)}
+                whole[0] = middle
+                swapped = {step: pltpu.roll(whole[step], fine_z, 1) for step in whole}
+
+                def beside(direction, step):
+                    if step == 0:
+                        return middle
+                    if direction == 1:
+                        return tall[offset + step : offset + step + block_rows]
+                    if direction == 2:
+                        return along_z(middle, step, fine_z)
+                    base = step // 2
+                    if step % 2 == 0:
+                        return whole[base]
+                    return jnp.where(low_half, swapped[base], swapped[base + 1])
+
+                rate = jnp.zeros_like(middle)
+                for direction in range(3):
+                    cells = [beside(direction, step) for step in range(-3, 4)]
+                    diffs = [cells[i + 1] - cells[i] for i in range(6)]
+                    speed = speeds[direction, major, pl.ds(start, block_rows)]
+                    rate = rate - speed * weno_upwind(diffs, speed)
+                moved_on = blend * (middle + STEP_FINE * rate)
+                if keep:
+                    moved_on = keep * level_in[major, rows] + moved_on
+                target[major, rows] = moved_on
+            return carry
+
+        lax.fori_loop(0, majors, one, 0)
+
+    section(level_in, stage_one, 0.0, 1.0)
+    section(stage_one, stage_two, 0.75, 0.25)
+    section(stage_two, stage_one, 1.0 / 3.0, 2.0 / 3.0)
+
+    pltpu.make_async_copy(marks_in, marks_in, take_sems.at[2]).wait()
+    mark_from = lax.broadcasted_iota(jnp.int32, (LANES, LANES), 0)
+    mark_to = lanes_of((LANES, LANES))
+    tile_z = plan["tile_z"]
+    tile_count = fine_z // tile_z
+    inside = pl.ds(offset, body)
+    spread_band = (mark_from == (mark_to % fine_z) // tile_z).astype(jnp.float32)
+    for part in range(halves):
+        marks = marks_in[part]
+        band = jnp.dot(marks, spread_band, preferred_element_type=jnp.float32)
+        for pair in range(pairs):
+            pick = jnp.logical_and(
+                mark_from == tile_count + 2 * pair + mark_to // fine_z, mark_to % fine_z == 0
+            ).astype(jnp.float32)
+            phase = jnp.dot(marks, pick, preferred_element_type=jnp.float32)
+            major = part * pairs + pair
+            banded = jnp.where(band > 0.5, stage_one[major, inside], level_in[major, inside])
+            shaped[major] = jnp.where(
+                phase > 1.5, SPREAD, jnp.where(phase > 0.5, -SPREAD, banded)
+            )
+
+    low_half = lanes_of((body, LANES)) < fine_z
+
+    def x_slope(ref, major):
+        here = pltpu.roll(ref[major], fine_z, 1)
+        up = pltpu.roll(ref[(major + 1) % majors], fine_z, 1)
+        down = pltpu.roll(ref[(major + majors - 1) % majors], fine_z, 1)
+        return 0.5 * (jnp.where(low_half, here, up) - jnp.where(low_half, down, here))
+
+    for major in range(majors):
+        level = shaped[major]
+        slope_x = x_slope(shaped, major)
+        slope_y = 0.5 * (along_rows(level, 1) - along_rows(level, -1))
+        slope_z = 0.5 * (along_z(level, 1, fine_z) - along_z(level, -1, fine_z))
+        inverse = lax.rsqrt(slope_x * slope_x + slope_y * slope_y + slope_z * slope_z + 1.0)
+        normals[0, major] = slope_x * inverse
+        normals[1, major] = slope_y * inverse
+        normals[2, major] = slope_z * inverse
+
+    core = slice(mark_margin, mark_margin + fine_chunk)
+    for major in range(majors):
+        normal_y, normal_z = normals[1, major], normals[2, major]
+        curvature = x_slope(normals.at[0], major)
+        curvature = curvature + 0.5 * (along_rows(normal_y, 1) - along_rows(normal_y, -1))
+        curvature = curvature + 0.5 * (
+            along_z(normal_z, 1, fine_z) - along_z(normal_z, -1, fine_z)
+        )
+        level = shaped[major]
+        delta_peak = jnp.exp(level * level * (-1.0 / (2.0 * SPREAD * SPREAD)))
+        strength = (SURFACE / (SPREAD * 2.5066282746310002)) * curvature * delta_peak
+        lane_spot = slice(major * LANES, (major + 1) * LANES)
+        for direction in range(3):
+            force = (normals[direction, major] * strength)[core]
+            packed[pl.ds(direction * fine_chunk, fine_chunk), lane_spot] = force
+        fraction = (0.5 + 0.5 * jnp.tanh(level * (1.0 / SPREAD)))[core]
+        packed[pl.ds(3 * fine_chunk, fine_chunk), lane_spot] = fraction
+
+    fine_from = lax.broadcasted_iota(jnp.int32, (majors * LANES, LANES), 0)
+    flow_to = lanes_of((majors * LANES, LANES))
+    fold_lanes = (
+        flow_to == (fine_from // LANES) * flow_z + (fine_from % fine_z) // 2
+    ).astype(jnp.float32)
+    folded = jnp.dot(
+        packed[...], fold_lanes, precision=EXACT, preferred_element_type=jnp.float32
+    )
+    fold_shape = (4 * flow_chunk, 4 * fine_chunk)
+    fold_rows = (
+        lanes_of(fold_shape) // 2 == lax.broadcasted_iota(jnp.int32, fold_shape, 0)
+    ).astype(jnp.float32)
+    means = 0.125 * jnp.dot(
+        fold_rows, folded, precision=EXACT, preferred_element_type=jnp.float32
+    )
+    for output in range(4):
+        mean = means[output * flow_chunk : (output + 1) * flow_chunk]
+        results[output] = moved[output] + STEP_FLOW * mean if output < 3 else mean
+
+    landing = pl.ds(pl.multiple_of(mine * flow_chunk, flow_chunk), flow_chunk)
+    for chunk in range(chunks):
+        push(results.at[chunk // halves], gathered.at[landing], chunk, ring, 3)
+    pltpu.make_async_copy(gathered, gathered, take_sems.at[3]).wait()
+    turned = gathered[...].T
+    outcome = turned[:share]
+    for part in range(1, halves):
+        outcome = jnp.where(half == part, turned[part * share : (part + 1) * share], outcome)
+    out_ref[...] = outcome
+    for condition, copy in sent:
+        if condition is None:
+            copy.wait_send()
+        else:
+            pl.when(condition)(copy.wait_send)
+
+
+def on_device_bricks(plan, flow_fields, level_set, band_tiles, nozzle_phase):
+    flow_z, flow_x, flow_y = flow_fields.shape[1:]
+    fine_z, fine_x, fine_y = level_set.shape[1:]
+    groups, halves = plan["groups"], plan["halves"]
+    chunks = groups * halves
+    fine_chunk, flow_chunk = fine_y // chunks, flow_y // chunks
+    tiles_z = band_tiles.shape[0]
+    plan = dict(
+        plan,
+        fine_chunk=fine_chunk,
+        flow_chunk=flow_chunk,
+        fine_z=fine_z,
+        flow_z=flow_z,
+        tile_z=fine_z // tiles_z,
+    )
+    flow = flow_fields[0].transpose(1, 0, 2).reshape(flow_x * flow_z, flow_y)
+    level = level_set[0].transpose(1, 0, 2).reshape(fine_x // 2, 2 * fine_z, fine_y)
+    band = jnp.repeat(band_tiles[:, 0, :], fine_y // band_tiles.shape[2], axis=1)
+    marks = jnp.concatenate([band, nozzle_phase], axis=0).astype(jnp.float32)
+    marks = jnp.pad(marks, ((0, LANES - marks.shape[0]), (0, 0)))
+    majors = fine_x // 2 * halves
+    body = fine_chunk + 2 * ROWS
+    tall = fine_chunk + 4 * ROWS
+    vmem = pl.BlockSpec(memory_space=pltpu.VMEM)
+
+    def room(*shape):
+        return pltpu.VMEM(shape, jnp.float32)
+
+    copies = 4 * chunks + 6
+    result = pl.pallas_call(
+        functools.partial(brick_kernel, plan),
+        out_shape=jax.ShapeDtypeStruct((flow_x * flow_z, flow_y), jnp.float32),
+        in_specs=[vmem] * 3,
+        out_specs=vmem,
+        scratch_shapes=[
+            room(flow_y, LANES),
+            room(fine_x // 2, fine_y, LANES),
+            room(fine_y, LANES),
+            room(groups, halves, flow_chunk + 2 * ROWS, LANES),
+            room(majors, tall, LANES),
+            room(halves, body, LANES),
+            room(3, majors, body, LANES),
+            room(majors, tall, LANES),
+            room(majors, tall, LANES),
+            room(majors, body, LANES),
+            room(3, majors, body, LANES),
+            room(4 * fine_chunk, majors * LANES),
+            room(4, flow_chunk, LANES),
+            room(flow_y, LANES),
+            pltpu.SemaphoreType.DMA((copies,)),
+            pltpu.SemaphoreType.DMA((4,)),
+        ],
+        compiler_params=pltpu.CompilerParams(
+            collective_id=0, has_side_effects=True, vmem_limit_bytes=32 * 1024 * 1024
+        ),
+        name="jet_step",
+    )(flow, level, marks)
+    return result.reshape(flow_x, flow_z, flow_y).transpose(1, 0, 2)[None]
+
+
 def solution(mesh):
     placed = (
         P("grp", None, "gx", "gy"),
@@ -243,6 +754,23 @@
         P(None, "gx", "gy"),
         P("gx", "gy"),
     )
+    plan = {"groups": mesh.shape["grp"], "halves": mesh.shape["gx"], "rings": mesh.shape["gy"]}
+
+    def on_device(flow_fields, level_set, band_tiles, nozzle_phase):
+        flow_z, flow_x, flow_y = flow_fields.shape[1:]
+        chunks = plan["groups"] * plan["halves"]
+        fits = (
+            plan["halves"] * flow_x * flow_z == LANES
+            and 2 * level_set.shape[1] == LANES
+            and flow_y == LANES
+            and flow_y % (chunks * 2 * ROWS) == 0
+            and band_tiles.shape[1] == 1
+            and plan["rings"] > 2
+        )
+        if fits:
+            return on_device_bricks(plan, flow_fields, level_set, band_tiles, nozzle_phase)
+        return on_device_general(flow_fields, level_set, band_tiles, nozzle_phase)
+
     return jax.shard_map(
         on_device, mesh=mesh, in_specs=placed, out_specs=P("grp", None, "gx", "gy"), check_vma=False
     )

time: 190 us -> 23.9 us (0.13)
  starting transfers between devices: 52.1 us -> 0 us
  waiting for transfers between devices: 48.1 us -> 0 us
  local copies, waits for them, and re-layouts: 46.5 us -> 2.37 us
  other arithmetic: 22.7 us -> 0.69 us
  Pallas kernels: 0 us -> 20.6 us
  between operations: 13.9 us -> 0.03 us
  blocking collectives: 6.47 us -> 0 us
    ppermute x40 -> x0, starting transfers between devices: 48.8 us -> none  [the longest x20 33.4 us: extended(): lax.ppermute(lax.slice_in_dim(block, 0, width, axis=dim), axis, backward)]
    ppermute x40 -> x0, waiting for transfers between devices: 44.2 us -> none  [the longest x20 31.5 us: extended(): lax.ppermute(lax.slice_in_dim(block, block.shape[dim] - width, None, axis...]
    reshape x7 -> x2, local copies, waits for them, and re-layouts: 34.3 us -> 0.73 us  [the longest x1 0.64 us: on_device_bricks(): return result.reshape(flow_x, flow_z, flow_y).transpose(1, 0, 2)[None]]
    pallas_call x0 -> x1, Pallas kernels: none -> 20.6 us  [on_device_bricks(): pl.pallas_call(functools.partial(brick_kernel, plan), out_shape=jax.Shape...]
    reduce_sum x4 -> x0, other arithmetic: 10.2 us -> none  [coarsen(): return jnp.sum(blocks, axis=(1, 3, 5)) * 0.125]
    broadcast_in_dim x7 -> x1, local copies, waits for them, and re-layouts: 8.38 us -> 0.76 us  [on_device_bricks(): jnp.repeat(band_tiles[:, 0, :], fine_y // band_tiles.shape[2], axis=1)]
    all_gather x1 -> x0, blocking collectives: 6.47 us -> none  [on_device(): gathered = lax.all_gather(flow_fields, 'grp', axis=0, tiled=True)]
    all_to_all x1 -> x0, waiting for transfers between devices: 3.88 us -> none  [spread_surface(): lax.all_to_all(quarter, 'grp', split_axis=0, concat_axis=1, tiled=True)]
  transfers between devices with their start and end apart: 42 -> 0, of which waited for: 25 -> 0; matrix products, arithmetic and copies ran while one was open for 34% -> 0% of each run, Pallas kernels for 0% -> 0%
where the time goes in v1:
time: 23.9 us; the launch traced here: 23.7 us
  Pallas kernels  20.6 us (86%)
  local copies, waits for them, and re-layouts  2.37 us (10%)
  other arithmetic  0.69 us (3%)
    pallas_call x1, Pallas kernels, on_device_bricks(): pl.pallas_call(functools.partial(brick_kernel, plan), out_shape=jax.Shape...  20.6 us
    transpose x1, local copies, waits for them, and re-layouts, on_device_bricks(): flow = flow_fields[0].transpose(1, 0, 2).reshape(flow_x * flow_z, flow_y)  0.8 us
    broadcast_in_dim x1, local copies, waits for them, and re-layouts, on_device_bricks(): jnp.repeat(band_tiles[:, 0, :], fine_y // band_tiles.shape[2], axis=1)  0.76 us
    convert_element_type x1, other arithmetic, on_device_bricks(): marks = jnp.concatenate([band, nozzle_phase], axis=0).astype(jnp.float32)  0.69 us
    reshape x1, local copies, waits for them, and re-layouts, on_device_bricks(): return result.reshape(flow_x, flow_z, flow_y).transpose(1, 0, 2)[None]  0.64 us

profile of v1, /device:TPU:0, one launch (start us, length us, event | category | flops | bytes accessed | tf_op | source)
XLA Modules:
  0.0 23.7 jit_solution(12945334647774336580)
XLA Ops:
  0.0 0.0 copy-start
  0.0 0.8 %copy.5 = f32[2,32,128]{2,1,0:T(8,128)S(1)} copy(f32[2,32,128]{2,0,1:T(2,128)} %bitcast.19) | data formatting | bytes 65536 | tf_op jit(solution)/shard_map/transpose | solution.py:705
  0.8 0.8 %broadcast_in_dim.6 = s32[8,16,16]{2,1,0:T(8,128)S(1)} broadcast(s32[8,16]{1,0:T(8,128)} %bitcast.20), dimensions={0,1} | broadcast | bytes 8704 | tf_op jit(solution)/shard_map/broadcast_in_dim | solution.py:707
  1.6 0.1 reshape.14
  1.7 0.7 %add_convert_fusion = f32[12,256]{1,0:T(8,128)S(1)} fusion(s32[4,256]{1,0:T(4,128)} %param.7, s32[8,256]{1,0:T(8,128)S(1)} %reshape.14), kind=kLoop, calls=%fused_computation.1 | loop fusion | flops 6144 | bytes 24576 | tf_op jit(solution)/shard_map/convert_element_type | solution.py:708
  2.4 0.0 copy-done
  2.4 0.1 copy.6
  2.4 20.6 %jet_step.1 = f32[64,128]{1,0:T(8,128)S(1)} custom-call(f32[64,128]{1,0:T(8,128)S(1)} %bitcast.16, f32[2,128,256]{2,1,0:T(8,128)S(1)} %bitcast.15, f32[128,256]{1,0:T(8,128)S(1)} %pad.4.marks_ref), custom_call_target="tpu_custom_call" | custom-call | tf_op jit(solution)/shard_map/jet_step/pallas_call | solution.py:719
  23.0 0.6 %copy.9 = f32[2,32,128]{2,0,1:T(2,128)} copy(f32[2,32,128]{2,1,0:T(8,128)S(1)} %bitcast.17) | data formatting | bytes 65536 | tf_op jit(solution)/shard_map/reshape | solution.py:747
  (1 shorter events, 0.0 us)
Async XLA Ops:
  0.0 2.4 %copy-start = (f32[1,64,4,256]{3,2,1,0:T(4,128)S(1)}, f32[1,64,4,256]{3,2,1,0:T(4,128)}, u32[]{:S(2)}) copy-start(f32[1,64,4,256]{3,2,1,0:T(4,128)} %param.5) | copy-start | bytes 786436

commit v2 on v1

--- a/solution.py
+++ b/solution.py
@@ -304,7 +304,8 @@
     plan,
     flow_ref,
     level_ref,
-    marks_ref,
+    band_ref,
+    phase_ref,
     out_ref,
     flow_turned,
     level_turned,
@@ -328,7 +329,8 @@
     fine_chunk, flow_chunk = plan["fine_chunk"], plan["flow_chunk"]
     fine_z, flow_z = plan["fine_z"], plan["flow_z"]
     fine_margin, mark_margin, flow_margin = 2 * ROWS, ROWS, ROWS
-    pairs = level_ref.shape[0]
+    fine_rows, flow_rows = chunks * fine_chunk, chunks * flow_chunk
+    pairs = level_ref.shape[1] // 2
     majors = pairs * halves
     group = lax.axis_index("grp")
     half = lax.axis_index("gx")
@@ -366,11 +368,29 @@
     @pl.when(group == groups - 1)
     def _():
         for pair in range(pairs):
-            level_turned[pair] = level_ref[pair].T
-
-    doubled = jnp.concatenate([flow_ref[...]] * halves, axis=0)
-    flow_turned[...] = doubled.T
-    marks_turned[...] = marks_ref[...].T
+            both = [level_ref[:, 2 * pair], level_ref[:, 2 * pair + 1]]
+            level_turned[pair] = jnp.concatenate(both, axis=0).T
+
+    columns = [flow_ref[:, column] for column in range(flow_ref.shape[1])]
+    flow_turned[...] = jnp.concatenate(columns * halves, axis=0).T
+    tiles_z, tiles_y = band_ref.shape
+    wide_shape = (tiles_y, fine_rows)
+    widen = (
+        lanes_of(wide_shape) // (fine_rows // tiles_y)
+        == lax.broadcasted_iota(jnp.int32, wide_shape, 0)
+    ).astype(jnp.float32)
+    wide_band = jnp.dot(
+        band_ref[...].astype(jnp.float32), widen, preferred_element_type=jnp.float32
+    )
+    spare = LANES - tiles_z - phase_ref.shape[0]
+    marks_turned[...] = jnp.concatenate(
+        [
+            wide_band,
+            phase_ref[...].astype(jnp.float32),
+            jnp.zeros((spare, fine_rows), jnp.float32),
+        ],
+        axis=0,
+    ).T
 
     pl.semaphore_wait(barrier, chunks + 1)
 
@@ -418,7 +438,6 @@
             0,
             holder,
         )
-    fine_rows = chunks * fine_chunk
     push(
         level_turned.at[:, pl.ds(fine_rows - fine_margin, fine_margin)],
         level_in.at[major_spot, pl.ds(0, fine_margin)],
@@ -444,7 +463,6 @@
             ring,
             1,
         )
-    flow_rows = chunks * flow_chunk
     push(
         flow_turned.at[pl.ds(flow_rows - flow_margin, flow_margin)],
         flow_in.at[group, half, pl.ds(0, flow_margin)],
@@ -702,11 +720,6 @@
         flow_z=flow_z,
         tile_z=fine_z // tiles_z,
     )
-    flow = flow_fields[0].transpose(1, 0, 2).reshape(flow_x * flow_z, flow_y)
-    level = level_set[0].transpose(1, 0, 2).reshape(fine_x // 2, 2 * fine_z, fine_y)
-    band = jnp.repeat(band_tiles[:, 0, :], fine_y // band_tiles.shape[2], axis=1)
-    marks = jnp.concatenate([band, nozzle_phase], axis=0).astype(jnp.float32)
-    marks = jnp.pad(marks, ((0, LANES - marks.shape[0]), (0, 0)))
     majors = fine_x // 2 * halves
     body = fine_chunk + 2 * ROWS
     tall = fine_chunk + 4 * ROWS
@@ -719,7 +732,7 @@
     result = pl.pallas_call(
         functools.partial(brick_kernel, plan),
         out_shape=jax.ShapeDtypeStruct((flow_x * flow_z, flow_y), jnp.float32),
-        in_specs=[vmem] * 3,
+        in_specs=[vmem] * 4,
         out_specs=vmem,
         scratch_shapes=[
             room(flow_y, LANES),
@@ -743,7 +756,7 @@
             collective_id=0, has_side_effects=True, vmem_limit_bytes=32 * 1024 * 1024
         ),
         name="jet_step",
-    )(flow, level, marks)
+    )(flow_fields[0], level_set[0], band_tiles[:, 0], nozzle_phase)
     return result.reshape(flow_x, flow_z, flow_y).transpose(1, 0, 2)[None]
 
 

time: 23.9 us -> 24.4 us (1.021)
  local copies, waits for them, and re-layouts: 2.37 us -> 3.72 us
  other arithmetic: 0.69 us -> 0 us
    unnamed x2 -> x8, local copies, waits for them, and re-layouts: 0.01 us -> 3.08 us
    transpose x2 -> x0, local copies, waits for them, and re-layouts: 0.86 us -> none  [the longest x1 0.8 us: on_device_bricks(): flow = flow_fields[0].transpose(1, 0, 2).reshape(flow_x * flow_z, flow_y)]
    broadcast_in_dim x1 -> x0, local copies, waits for them, and re-layouts: 0.76 us -> none  [on_device_bricks(): jnp.repeat(band_tiles[:, 0, :], fine_y // band_tiles.shape[2], axis=1)]
    convert_element_type x1 -> x0, other arithmetic: 0.69 us -> none  [on_device_bricks(): marks = jnp.concatenate([band, nozzle_phase], axis=0).astype(jnp.float32)]
where the time goes in v2:
time: 24.4 us; the launch traced here: 24.2 us
  Pallas kernels  20.4 us (84%)
  local copies, waits for them, and re-layouts  3.72 us (15%)
    pallas_call x1, Pallas kernels, on_device_bricks(): pl.pallas_call(functools.partial(brick_kernel, plan), out_shape=jax.Shape...  20.4 us
    unnamed x8, local copies, waits for them, and re-layouts  3.08 us
    reshape x1, local copies, waits for them, and re-layouts, on_device_bricks(): return result.reshape(flow_x, flow_z, flow_y).transpose(1, 0, 2)[None]  0.64 us

profile of v2, /device:TPU:0, one launch (start us, length us, event | category | flops | bytes accessed | tf_op | source)
XLA Modules:
  0.0 24.2 jit_solution(15866620450568024190)
XLA Ops:
  0.0 0.0 copy-start.2
  0.0 0.7 %copy-done.2 = s32[8,1,16]{2,1,0:T(1,128)S(1)} copy-done((s32[8,1,16]{2,1,0:T(1,128)S(1)}, s32[8,1,16]{2,1,0:T(1,128)}, u32[]{:S(2)}) %copy-start.2) | copy-done | bytes 536
  0.7 0.0 copy-start
  0.7 0.9 %copy-done = f32[1,64,4,256]{3,2,1,0:T(4,128)S(1)} copy-done((f32[1,64,4,256]{3,2,1,0:T(4,128)S(1)}, f32[1,64,4,256]{3,2,1,0:T(4,128)}, u32[]{:S(2)}) %copy-start) | copy-done | bytes 262168
  1.6 0.0 copy-start.1
  1.6 0.8 %copy-done.1 = f32[1,32,2,128]{3,2,1,0:T(2,128)S(1)} copy-done((f32[1,32,2,128]{3,2,1,0:T(2,128)S(1)}, f32[1,32,2,128]{3,2,1,0:T(2,128)}, u32[]{:S(2)}) %copy-start.1) | copy-done | bytes 32792
  2.4 0.0 copy-start.3
  2.4 0.7 %copy-done.3 = s32[4,256]{1,0:T(4,128)S(1)} copy-done((s32[4,256]{1,0:T(4,128)S(1)}, s32[4,256]{1,0:T(4,128)}, u32[]{:S(2)}) %copy-start.3) | copy-done | bytes 4120
  3.1 20.4 %jet_step.1 = f32[64,128]{1,0:T(8,128)S(1)} custom-call(f32[32,2,128]{2,1,0:T(2,128)S(1)} %bitcast.11, f32[64,4,256]{2,1,0:T(4,128)S(1)} %bitcast.9, s32[8,16]{1,0:T(8,128)S(1)} %bitcast.12, s32[4,256]{1,0:T(4,128)S(1)} %copy-done.3), custom_call_target="tpu_custom_call" | custom-call | tf_op jit(solution)/shard_map/jet_step/pallas_call | solution.py:732
  23.5 0.6 %copy.7 = f32[2,32,128]{2,0,1:T(2,128)} copy(f32[2,32,128]{2,1,0:T(8,128)S(1)} %bitcast.10) | data formatting | bytes 65536 | tf_op jit(solution)/shard_map/reshape | solution.py:760
Async XLA Ops:
  0.0 0.7 %copy-start.2 = (s32[8,1,16]{2,1,0:T(1,128)S(1)}, s32[8,1,16]{2,1,0:T(1,128)}, u32[]{:S(2)}) copy-start(s32[8,1,16]{2,1,0:T(1,128)} %param.6) | copy-start | bytes 1540
  0.7 0.9 %copy-start = (f32[1,64,4,256]{3,2,1,0:T(4,128)S(1)}, f32[1,64,4,256]{3,2,1,0:T(4,128)}, u32[]{:S(2)}) copy-start(f32[1,64,4,256]{3,2,1,0:T(4,128)} %param.5) | copy-start | bytes 786436
  1.6 0.8 %copy-start.1 = (f32[1,32,2,128]{3,2,1,0:T(2,128)S(1)}, f32[1,32,2,128]{3,2,1,0:T(2,128)}, u32[]{:S(2)}) copy-start(f32[1,32,2,128]{3,2,1,0:T(2,128)} %param.4) | copy-start | bytes 98308
  2.4 0.7 %copy-start.3 = (s32[4,256]{1,0:T(4,128)S(1)}, s32[4,256]{1,0:T(4,128)}, u32[]{:S(2)}) copy-start(s32[4,256]{1,0:T(4,128)} %phase_ref.1) | copy-start | bytes 12292

commit v3 on v2

--- a/solution.py
+++ b/solution.py
@@ -302,11 +302,15 @@
 
 def brick_kernel(
     plan,
+    flow_far,
+    level_far,
+    band_far,
+    phase_far,
+    out_ref,
     flow_ref,
     level_ref,
     band_ref,
     phase_ref,
-    out_ref,
     flow_turned,
     level_turned,
     marks_turned,
@@ -323,6 +327,7 @@
     gathered,
     send_sems,
     take_sems,
+    load_sems,
 ):
     groups, halves, rings = plan["groups"], plan["halves"], plan["rings"]
     chunks = groups * halves
@@ -340,6 +345,16 @@
     mine = group * halves + half
     last = chunks - 1
 
+    holder = group == groups - 1
+    load_level = pltpu.make_async_copy(level_far, level_ref, load_sems.at[0])
+    load_flow = pltpu.make_async_copy(flow_far, flow_ref, load_sems.at[1])
+    load_band = pltpu.make_async_copy(band_far, band_ref, load_sems.at[2])
+    load_phase = pltpu.make_async_copy(phase_far, phase_ref, load_sems.at[3])
+    pl.when(holder)(load_level.start)
+    load_flow.start()
+    load_band.start()
+    load_phase.start()
+
     barrier = pltpu.get_barrier_semaphore()
 
     def greet(target_group, target_half, target_ring):
@@ -365,14 +380,18 @@
         def _(tg=tg, th=th):
             greet(tg, th, after)
 
-    @pl.when(group == groups - 1)
+    @pl.when(holder)
     def _():
+        load_level.wait()
         for pair in range(pairs):
             both = [level_ref[:, 2 * pair], level_ref[:, 2 * pair + 1]]
             level_turned[pair] = jnp.concatenate(both, axis=0).T
 
+    load_flow.wait()
     columns = [flow_ref[:, column] for column in range(flow_ref.shape[1])]
     flow_turned[...] = jnp.concatenate(columns * halves, axis=0).T
+    load_band.wait()
+    load_phase.wait()
     tiles_z, tiles_y = band_ref.shape
     wide_shape = (tiles_y, fine_rows)
     widen = (
@@ -426,7 +445,6 @@
             pl.when(far)(remote.start)
         sent.append((far, remote))
 
-    holder = group == groups - 1
     major_spot = pl.ds(half * pairs, pairs)
     for chunk in range(chunks):
         start, count, spot = window(chunk, chunks, fine_chunk, fine_margin)
@@ -732,9 +750,13 @@
     result = pl.pallas_call(
         functools.partial(brick_kernel, plan),
         out_shape=jax.ShapeDtypeStruct((flow_x * flow_z, flow_y), jnp.float32),
-        in_specs=[vmem] * 4,
+        in_specs=[pl.BlockSpec(memory_space=pltpu.HBM)] * 4,
         out_specs=vmem,
         scratch_shapes=[
+            room(flow_z, flow_x, flow_y),
+            room(fine_z, fine_x, fine_y),
+            pltpu.VMEM((band_tiles.shape[0], band_tiles.shape[2]), band_tiles.dtype),
+            pltpu.VMEM(nozzle_phase.shape, nozzle_phase.dtype),
             room(flow_y, LANES),
             room(fine_x // 2, fine_y, LANES),
             room(fine_y, LANES),
@@ -751,9 +773,10 @@
             room(flow_y, LANES),
             pltpu.SemaphoreType.DMA((copies,)),
             pltpu.SemaphoreType.DMA((4,)),
+            pltpu.SemaphoreType.DMA((4,)),
         ],
         compiler_params=pltpu.CompilerParams(
-            collective_id=0, has_side_effects=True, vmem_limit_bytes=32 * 1024 * 1024
+            collective_id=0, has_side_effects=True, vmem_limit_bytes=60 * 1024 * 1024
         ),
         name="jet_step",
     )(flow_fields[0], level_set[0], band_tiles[:, 0], nozzle_phase)

time: 24.4 us -> 22.8 us (0.934)
  local copies, waits for them, and re-layouts: 3.72 us -> 1.4 us
  Pallas kernels: 20.4 us -> 21.1 us
    unnamed x8 -> x0, local copies, waits for them, and re-layouts: 3.08 us -> none
    reshape x1, local copies, waits for them, and re-layouts: 0.64 us -> 1.4 us  [on_device_bricks(): return result.reshape(flow_x, flow_z, flow_y).transpose(1, 0, 2)[None]]
    pallas_call x1, Pallas kernels: 20.4 us -> 21.1 us  [on_device_bricks(): pl.pallas_call(functools.partial(brick_kernel, plan), out_shape=jax.Shape...]
where the time goes in v3:
time: 22.8 us; the launch traced here: 22.6 us
  Pallas kernels  21.1 us (93%)
  local copies, waits for them, and re-layouts  1.4 us (6%)
    pallas_call x1, Pallas kernels, on_device_bricks(): pl.pallas_call(functools.partial(brick_kernel, plan), out_shape=jax.Shape...  21.1 us
    reshape x1, local copies, waits for them, and re-layouts, on_device_bricks(): return result.reshape(flow_x, flow_z, flow_y).transpose(1, 0, 2)[None]  1.4 us

profile of v3, /device:TPU:0, one launch (start us, length us, event | category | flops | bytes accessed | tf_op | source)
XLA Modules:
  0.0 22.6 jit_solution(9113188045040634360)
XLA Ops:
  0.0 21.1 %jet_step.1 = f32[64,128]{1,0:T(8,128)} custom-call(f32[32,2,128]{2,1,0:T(2,128)} %bitcast.11, f32[64,4,256]{2,1,0:T(4,128)} %bitcast.9, s32[8,16]{1,0:T(8,128)} %bitcast.12, s32[4,256]{1,0:T(4,128)} %phase_far.1), custom_call_target="tpu_custom_call" | custom-call | tf_op jit(solution)/shard_map/jet_step/pallas_call | solution.py:750
  21.1 1.4 %copy.7 = f32[2,32,128]{2,0,1:T(2,128)} copy(f32[2,32,128]{2,1,0:T(8,128)} %bitcast.10) | data formatting | bytes 65536 | tf_op jit(solution)/shard_map/reshape | solution.py:783

commit v4 on v3

--- a/solution.py
+++ b/solution.py
@@ -264,33 +264,35 @@
     return pltpu.roll(block, (-offset) % block.shape[0], 0)
 
 
-def weno_upwind(diffs, speed):
-    forward = speed >= 0.0
-    one = jnp.where(forward, diffs[0], diffs[5])
-    two = jnp.where(forward, diffs[1], diffs[4])
-    three = jnp.where(forward, diffs[2], diffs[3])
-    four = jnp.where(forward, diffs[3], diffs[2])
-    five = jnp.where(forward, diffs[4], diffs[1])
-    step_a = two - one
-    step_b = three - two
-    step_c = four - three
-    step_d = five - four
+def inverse_of(block):
+    rough = pl.reciprocal(block, approx=True)
+    return rough * (2.0 - block * rough)
+
+
+def weno_flux(bends, near, speed, forward, pace):
+    step_a = jnp.where(forward, bends[0], bends[4])
+    step_b = jnp.where(forward, bends[1], bends[3])
+    step_c = bends[2]
+    step_d = jnp.where(forward, bends[3], bends[1])
+    three = jnp.where(forward, near[0], near[1])
 
     def weight(curve, slope):
-        rough = (WENO_EPS * 12.0 / 13.0) + curve * curve + (3.0 / 13.0) * (slope * slope)
-        inverse = 1.0 / rough
+        inverse = inverse_of(
+            (WENO_EPS * 12.0 / 13.0) + curve * curve + (3.0 / 13.0) * (slope * slope)
+        )
         return inverse * inverse
 
+    triple_c = 3.0 * step_c
     weight_one = weight(step_b - step_a, 3.0 * step_b - step_a)
     weight_two = 6.0 * weight(step_c - step_b, step_c + step_b)
-    weight_three = 3.0 * weight(step_d - step_c, 3.0 * step_c - step_d)
+    weight_three = 3.0 * weight(step_d - step_c, triple_c - step_d)
     mixed = (
         weight_one * (5.0 * step_b - 2.0 * step_a)
         + weight_two * (step_b + 2.0 * step_c)
-        + weight_three * (4.0 * step_c - step_d)
+        + weight_three * (step_c + triple_c - step_d)
     )
     total = weight_one + weight_two + weight_three
-    return three + mixed / (6.0 * total)
+    return speed * three + (pace * mixed) * inverse_of(total)
 
 
 def window(index, count, chunk, margin):
@@ -615,10 +617,24 @@
 
                 rate = jnp.zeros_like(middle)
                 for direction in range(3):
-                    cells = [beside(direction, step) for step in range(-3, 4)]
-                    diffs = [cells[i + 1] - cells[i] for i in range(6)]
+                    if direction == 2:
+                        first = along_z(middle, 1, fine_z) - middle
+                        behind = along_z(first, -1, fine_z)
+                        bend = first - behind
+                        bends = [
+                            along_z(bend, step, fine_z) if step else bend
+                            for step in (-2, -1, 0, 1, 2)
+                        ]
+                        near = (behind, first)
+                    else:
+                        cells = [beside(direction, step) for step in range(-3, 4)]
+                        diffs = [cells[i + 1] - cells[i] for i in range(6)]
+                        bends = [diffs[i + 1] - diffs[i] for i in range(5)]
+                        near = (diffs[2], diffs[3])
                     speed = speeds[direction, major, pl.ds(start, block_rows)]
-                    rate = rate - speed * weno_upwind(diffs, speed)
+                    forward = speed >= 0.0
+                    pace = jnp.abs(speed) * (1.0 / 6.0)
+                    rate = rate - weno_flux(bends, near, speed, forward, pace)
                 moved_on = blend * (middle + STEP_FINE * rate)
                 if keep:
                     moved_on = keep * level_in[major, rows] + moved_on

time: 22.8 us -> 23.4 us (1.026)
  Pallas kernels: 21.1 us -> 21.8 us
    pallas_call x1, Pallas kernels: 21.1 us -> 21.8 us  [on_device_bricks(): pl.pallas_call(functools.partial(brick_kernel, plan), out_shape=jax.Shape...]
where the time goes in v4:
time: 23.4 us; the launch traced here: 23.2 us
  Pallas kernels  21.8 us (93%)
  local copies, waits for them, and re-layouts  1.4 us (6%)
    pallas_call x1, Pallas kernels, on_device_bricks(): pl.pallas_call(functools.partial(brick_kernel, plan), out_shape=jax.Shape...  21.8 us
    reshape x1, local copies, waits for them, and re-layouts, on_device_bricks(): return result.reshape(flow_x, flow_z, flow_y).transpose(1, 0, 2)[None]  1.4 us

profile of v4, /device:TPU:0, one launch (start us, length us, event | category | flops | bytes accessed | tf_op | source)
XLA Modules:
  0.0 23.2 jit_solution(6641246224034834380)
XLA Ops:
  0.0 21.8 %jet_step.1 = f32[64,128]{1,0:T(8,128)} custom-call(f32[32,2,128]{2,1,0:T(2,128)} %bitcast.11, f32[64,4,256]{2,1,0:T(4,128)} %bitcast.9, s32[8,16]{1,0:T(8,128)} %bitcast.12, s32[4,256]{1,0:T(4,128)} %phase_far.1), custom_call_target="tpu_custom_call" | custom-call | tf_op jit(solution)/shard_map/jet_step/pallas_call | solution.py:766
  21.8 1.4 %copy.7 = f32[2,32,128]{2,0,1:T(2,128)} copy(f32[2,32,128]{2,1,0:T(8,128)} %bitcast.10) | data formatting | bytes 65536 | tf_op jit(solution)/shard_map/reshape | solution.py:799

commit v5 on v4

--- a/solution.py
+++ b/solution.py
@@ -590,34 +590,46 @@
     block_rows = 2 * ROWS
 
     def section(current, target, keep, blend):
-        def one(major, carry):
-            def far_major(step):
-                return lax.rem(major + majors + step, majors)
-
-            for start in range(0, body, block_rows):
-                rows = pl.ds(offset + start, block_rows)
-                tall = current[major, pl.ds(start, block_rows + 2 * offset)]
-                middle = tall[offset : offset + block_rows]
-                low_half = lanes_of(middle.shape) < fine_z
-                whole = {step: current[far_major(step), rows] for step in (-2, -1, 1, 2)}
-                whole[0] = middle
-                swapped = {step: pltpu.roll(whole[step], fine_z, 1) for step in whole}
-
-                def beside(direction, step):
-                    if step == 0:
-                        return middle
-                    if direction == 1:
-                        return tall[offset + step : offset + step + block_rows]
-                    if direction == 2:
-                        return along_z(middle, step, fine_z)
-                    base = step // 2
-                    if step % 2 == 0:
-                        return whole[base]
-                    return jnp.where(low_half, swapped[base], swapped[base + 1])
-
+        for start in range(0, body, block_rows):
+            rows = pl.ds(offset + start, block_rows)
+            span = pl.ds(start, block_rows + 2 * offset)
+            here = pl.ds(start, block_rows)
+            talls = [current[major, span] for major in range(majors)]
+            whole = [tall[offset : offset + block_rows] for tall in talls]
+            swapped = [pltpu.roll(block, fine_z, 1) for block in whole]
+            low_half = lanes_of(whole[0].shape) < fine_z
+            crossed = [
+                jnp.where(low_half, swapped[major], swapped[(major + 1) % majors])
+                for major in range(majors)
+            ]
+            rises = [crossed[major] - whole[major] for major in range(majors)]
+            falls = [whole[(major + 1) % majors] - crossed[major] for major in range(majors)]
+            humps = [falls[major] - rises[major] for major in range(majors)]
+            dips = [rises[(major + 1) % majors] - falls[major] for major in range(majors)]
+            for major in range(majors):
+                middle = whole[major]
                 rate = jnp.zeros_like(middle)
                 for direction in range(3):
-                    if direction == 2:
+                    if direction == 0:
+                        left, far = (major - 1) % majors, (major - 2) % majors
+                        bends = [
+                            dips[far],
+                            humps[left],
+                            dips[left],
+                            humps[major],
+                            dips[major],
+                        ]
+                        near = (falls[left], rises[major])
+                    elif direction == 1:
+                        tall = talls[major]
+                        cells = [
+                            tall[offset + step : offset + step + block_rows]
+                            for step in range(-3, 4)
+                        ]
+                        diffs = [cells[i + 1] - cells[i] for i in range(6)]
+                        bends = [diffs[i + 1] - diffs[i] for i in range(5)]
+                        near = (diffs[2], diffs[3])
+                    else:
                         first = along_z(middle, 1, fine_z) - middle
                         behind = along_z(first, -1, fine_z)
                         bend = first - behind
@@ -626,12 +638,7 @@
                             for step in (-2, -1, 0, 1, 2)
                         ]
                         near = (behind, first)
-                    else:
-                        cells = [beside(direction, step) for step in range(-3, 4)]
-                        diffs = [cells[i + 1] - cells[i] for i in range(6)]
-                        bends = [diffs[i + 1] - diffs[i] for i in range(5)]
-                        near = (diffs[2], diffs[3])
-                    speed = speeds[direction, major, pl.ds(start, block_rows)]
+                    speed = speeds[direction, major, here]
                     forward = speed >= 0.0
                     pace = jnp.abs(speed) * (1.0 / 6.0)
                     rate = rate - weno_flux(bends, near, speed, forward, pace)
@@ -639,9 +646,6 @@
                 if keep:
                     moved_on = keep * level_in[major, rows] + moved_on
                 target[major, rows] = moved_on
-            return carry
-
-        lax.fori_loop(0, majors, one, 0)
 
     section(level_in, stage_one, 0.0, 1.0)
     section(stage_one, stage_two, 0.75, 0.25)
@@ -731,7 +735,9 @@
     outcome = turned[:share]
     for part in range(1, halves):
         outcome = jnp.where(half == part, turned[part * share : (part + 1) * share], outcome)
-    out_ref[...] = outcome
+    depth = share // out_ref.shape[1]
+    for column in range(out_ref.shape[1]):
+        out_ref[:, column] = outcome[column * depth : (column + 1) * depth]
     for condition, copy in sent:
         if condition is None:
             copy.wait_send()
@@ -765,7 +771,7 @@
     copies = 4 * chunks + 6
     result = pl.pallas_call(
         functools.partial(brick_kernel, plan),
-        out_shape=jax.ShapeDtypeStruct((flow_x * flow_z, flow_y), jnp.float32),
+        out_shape=jax.ShapeDtypeStruct((flow_z, flow_x, flow_y), jnp.float32),
         in_specs=[pl.BlockSpec(memory_space=pltpu.HBM)] * 4,
         out_specs=vmem,
         scratch_shapes=[
@@ -796,7 +802,7 @@
         ),
         name="jet_step",
     )(flow_fields[0], level_set[0], band_tiles[:, 0], nozzle_phase)
-    return result.reshape(flow_x, flow_z, flow_y).transpose(1, 0, 2)[None]
+    return result[None]
 
 
 def solution(mesh):

time: 23.4 us -> 24.9 us (1.064)
  Pallas kernels: 21.8 us -> 23.3 us
    pallas_call x1, Pallas kernels: 21.8 us -> 23.3 us  [on_device_bricks(): pl.pallas_call(functools.partial(brick_kernel, plan), out_shape=jax.Shape...]
    reshape x1 -> x0, local copies, waits for them, and re-layouts: 1.4 us -> none  [on_device_bricks(): return result.reshape(flow_x, flow_z, flow_y).transpose(1, 0, 2)[None]]
    unnamed x0 -> x1, local copies, waits for them, and re-layouts: none -> 1.38 us
where the time goes in v5:
time: 24.9 us; the launch traced here: 24.7 us
  Pallas kernels  23.3 us (94%)
  local copies, waits for them, and re-layouts  1.38 us (6%)
    pallas_call x1, Pallas kernels, on_device_bricks(): pl.pallas_call(functools.partial(brick_kernel, plan), out_shape=jax.Shape...  23.3 us
    unnamed x1, local copies, waits for them, and re-layouts  1.38 us

profile of v5, /device:TPU:0, one launch (start us, length us, event | category | flops | bytes accessed | tf_op | source)
XLA Modules:
  0.0 24.7 jit_solution(8347384681318797800)
XLA Ops:
  0.0 23.3 %jet_step.1 = f32[32,2,128]{2,1,0:T(2,128)} custom-call(f32[32,2,128]{2,1,0:T(2,128)} %bitcast.6, f32[64,4,256]{2,1,0:T(4,128)} %bitcast.4, s32[8,16]{1,0:T(8,128)} %bitcast.7, s32[4,256]{1,0:T(4,128)} %phase_far.1), custom_call_target="tpu_custom_call" | custom-call | tf_op jit(solution)/shard_map/jet_step/pallas_call | solution.py:772
  23.3 1.4 %copy.6 = f32[1,32,2,128]{3,2,1,0:T(2,128)} copy(f32[1,32,2,128]{3,2,1,0:T(2,128)} %bitcast.5) | data formatting | bytes 65536

commit v6 on v4

--- a/solution.py
+++ b/solution.py
@@ -295,13 +295,6 @@
     return speed * three + (pace * mixed) * inverse_of(total)
 
 
-def window(index, count, chunk, margin):
-    low = index * chunk - margin
-    high = (index + 1) * chunk + margin
-    start, stop = max(low, 0), min(high, count * chunk)
-    return start, stop - start, start - low
-
-
 def brick_kernel(
     plan,
     flow_far,
@@ -317,14 +310,14 @@
     level_turned,
     marks_turned,
     flow_in,
-    level_in,
+    stages,
     marks_in,
     speeds,
-    stage_one,
-    stage_two,
+    fields,
+    pushes,
     shaped,
     normals,
-    packed,
+    folded,
     results,
     gathered,
     send_sems,
@@ -367,20 +360,24 @@
             device_id_type=MESH,
         )
 
-    for chunk in range(chunks):
-        tg, th = chunk // halves, chunk % halves
+    def greet_all(chunk, carry):
+        tg, th = chunk // halves, lax.rem(chunk, halves)
 
         @pl.when(mine != chunk)
-        def _(tg=tg, th=th):
+        def _():
             greet(tg, th, ring)
 
         @pl.when(mine == 0)
-        def _(tg=tg, th=th):
+        def _():
             greet(tg, th, before)
 
         @pl.when(mine == last)
-        def _(tg=tg, th=th):
+        def _():
             greet(tg, th, after)
+
+        return carry
+
+    lax.fori_loop(0, chunks, greet_all, 0)
 
     @pl.when(holder)
     def _():
@@ -415,131 +412,159 @@
 
     pl.semaphore_wait(barrier, chunks + 1)
 
-    sent = []
-
-    def push(source, target, chunk, ring_to, take, condition=None):
-        tg, th = chunk // halves, chunk % halves
-        slot = len(sent)
+    def move(kind, slot, source, target, chunk, ring_to, condition, finish):
+        tg, th = chunk // halves, lax.rem(chunk, halves)
+        near = ring_to is ring
+        far = jnp.logical_and(condition, mine != chunk) if near else condition
         remote = pltpu.make_async_remote_copy(
             src_ref=source,
             dst_ref=target,
-            send_sem=send_sems.at[slot],
-            recv_sem=take_sems.at[take],
+            send_sem=send_sems.at[kind * (chunks + 2) + slot],
+            recv_sem=take_sems.at[kind],
             device_id=(tg, th, ring_to),
             device_id_type=MESH,
         )
-        near = ring_to is ring
-        far = mine != chunk if near else None
-        if condition is not None:
-            far = condition if far is None else jnp.logical_and(condition, far)
-        if near:
-            here = mine == chunk
-            if condition is not None:
-                here = jnp.logical_and(condition, here)
-
-            @pl.when(here)
+        pl.when(far)(remote.wait_send if finish else remote.start)
+        if near and not finish:
+
+            @pl.when(jnp.logical_and(condition, mine == chunk))
             def _():
-                pltpu.make_async_copy(source, target, take_sems.at[take]).start()
-
-        if far is None:
-            remote.start()
-        else:
-            pl.when(far)(remote.start)
-        sent.append((far, remote))
+                pltpu.make_async_copy(source, target, take_sems.at[kind]).start()
+
+    def spread(kind, source, target, chunk_rows, margin, condition, finish):
+        total = chunks * chunk_rows
+        wide = chunk_rows + 2 * margin
+        first, final = jnp.int32(0), jnp.int32(last)
+        side = wide - margin
+        move(
+            kind,
+            0,
+            source(pl.ds(0, side)),
+            target(pl.ds(margin, side)),
+            first,
+            ring,
+            condition(first),
+            finish,
+        )
+
+        def inner(chunk, carry):
+            start = pl.multiple_of(chunk * chunk_rows - margin, ROWS)
+            move(
+                kind,
+                chunk,
+                source(pl.ds(start, wide)),
+                target(pl.ds(0, wide)),
+                chunk,
+                ring,
+                condition(chunk),
+                finish,
+            )
+            return carry
+
+        lax.fori_loop(1, last, inner, 0)
+        move(
+            kind,
+            last,
+            source(pl.ds(total - side, side)),
+            target(pl.ds(0, side)),
+            final,
+            ring,
+            condition(final),
+            finish,
+        )
+        move(
+            kind,
+            chunks,
+            source(pl.ds(total - margin, margin)),
+            target(pl.ds(0, margin)),
+            first,
+            after,
+            condition(first),
+            finish,
+        )
+        move(
+            kind,
+            chunks + 1,
+            source(pl.ds(0, margin)),
+            target(pl.ds(margin + chunk_rows, margin)),
+            final,
+            before,
+            condition(final),
+            finish,
+        )
 
     major_spot = pl.ds(half * pairs, pairs)
-    for chunk in range(chunks):
-        start, count, spot = window(chunk, chunks, fine_chunk, fine_margin)
-        push(
-            level_turned.at[:, pl.ds(start, count)],
-            level_in.at[major_spot, pl.ds(spot, count)],
-            chunk,
-            ring,
+
+    def spread_level(finish):
+        spread(
             0,
-            holder,
-        )
-    push(
-        level_turned.at[:, pl.ds(fine_rows - fine_margin, fine_margin)],
-        level_in.at[major_spot, pl.ds(0, fine_margin)],
-        0,
-        after,
-        0,
-        holder,
-    )
-    push(
-        level_turned.at[:, pl.ds(0, fine_margin)],
-        level_in.at[major_spot, pl.ds(fine_margin + fine_chunk, fine_margin)],
-        last,
-        before,
-        0,
-        holder,
-    )
-    for chunk in range(chunks):
-        start, count, spot = window(chunk, chunks, flow_chunk, flow_margin)
-        push(
-            flow_turned.at[pl.ds(start, count)],
-            flow_in.at[group, half, pl.ds(spot, count)],
-            chunk,
-            ring,
+            lambda rows: level_turned.at[:, rows],
+            lambda rows: stages.at[0, major_spot, rows],
+            fine_chunk,
+            fine_margin,
+            lambda chunk: holder,
+            finish,
+        )
+
+    def spread_flow(finish):
+        spread(
             1,
-        )
-    push(
-        flow_turned.at[pl.ds(flow_rows - flow_margin, flow_margin)],
-        flow_in.at[group, half, pl.ds(0, flow_margin)],
-        0,
-        after,
-        1,
-    )
-    push(
-        flow_turned.at[pl.ds(0, flow_margin)],
-        flow_in.at[group, half, pl.ds(flow_margin + flow_chunk, flow_margin)],
-        last,
-        before,
-        1,
-    )
-    for chunk in range(chunks):
-        start, count, spot = window(chunk, chunks, fine_chunk, mark_margin)
-        push(
-            marks_turned.at[pl.ds(start, count)],
-            marks_in.at[half, pl.ds(spot, count)],
-            chunk,
-            ring,
+            lambda rows: flow_turned.at[rows],
+            lambda rows: flow_in.at[group, half, rows],
+            flow_chunk,
+            flow_margin,
+            lambda chunk: group >= 0,
+            finish,
+        )
+
+    def spread_marks(finish):
+        spread(
             2,
-            group == chunk // halves,
-        )
-    push(
-        marks_turned.at[pl.ds(fine_rows - mark_margin, mark_margin)],
-        marks_in.at[half, pl.ds(0, mark_margin)],
-        0,
-        after,
-        2,
-        group == 0,
-    )
-    push(
-        marks_turned.at[pl.ds(0, mark_margin)],
-        marks_in.at[half, pl.ds(mark_margin + fine_chunk, mark_margin)],
-        last,
-        before,
-        2,
-        group == groups - 1,
-    )
+            lambda rows: marks_turned.at[rows],
+            lambda rows: marks_in.at[half, rows],
+            fine_chunk,
+            mark_margin,
+            lambda chunk: group == chunk // halves,
+            finish,
+        )
+
+    landing = pl.ds(pl.multiple_of(mine * flow_chunk, flow_chunk), flow_chunk)
+
+    def spread_results(finish):
+        def one(chunk, carry):
+            move(
+                3,
+                chunk,
+                results.at[chunk // halves],
+                gathered.at[landing],
+                chunk,
+                ring,
+                group >= 0,
+                finish,
+            )
+            return carry
+
+        lax.fori_loop(0, chunks, one, 0)
+
+    pl.when(holder)(lambda: spread_level(False))
+    spread_flow(False)
+    spread_marks(False)
 
     body = fine_chunk + 2 * mark_margin
     offset = fine_margin - mark_margin
     edge = jnp.zeros((majors, offset, LANES), jnp.float32)
-    for stage in (stage_one, stage_two):
-        stage[:, pl.ds(0, offset)] = edge
-        stage[:, pl.ds(offset + body, offset)] = edge
+    for stage in (1, 2):
+        stages[stage, :, pl.ds(0, offset)] = edge
+        stages[stage, :, pl.ds(offset + body, offset)] = edge
 
     pltpu.make_async_copy(flow_in, flow_in, take_sems.at[1]).wait()
     share = LANES // halves
-    fields = []
     flow_lane = lanes_of((flow_chunk + 2 * flow_margin, LANES))
     for field in range(groups):
         merged = flow_in[field, 0]
         for part in range(1, halves):
             merged = jnp.where(flow_lane >= part * share, flow_in[field, part], merged)
-        fields.append(merged)
+        fields[field] = merged
 
     from_flow = lax.broadcasted_iota(jnp.int32, (LANES, majors * LANES), 0)
     to_fine = lanes_of((LANES, majors * LANES))
@@ -551,13 +576,17 @@
         == lax.broadcasted_iota(jnp.int32, (body, flow_window), 0) // 2
         + (flow_margin - mark_margin // 2)
     ).astype(jnp.float32)
-    for direction in range(3):
+
+    def spread_speed(direction, carry):
         tall = jnp.dot(
             spread_rows, fields[direction], precision=EXACT, preferred_element_type=jnp.float32
         )
         wide = jnp.dot(tall, spread_lanes, precision=EXACT, preferred_element_type=jnp.float32)
         for major in range(majors):
             speeds[direction, major] = wide[:, major * LANES : (major + 1) * LANES]
+        return carry
+
+    lax.fori_loop(0, 3, spread_speed, 0)
 
     def flow_beside(block, direction, step):
         if direction == 0:
@@ -569,37 +598,49 @@
     def flow_slope(block, direction):
         return 0.5 * (flow_beside(block, direction, 1) - flow_beside(block, direction, -1))
 
-    moved = []
-    for component in range(3):
+    for direction in range(3):
+        pushes[direction] = flow_slope(fields[3], direction)
+
+    def relax(component, carry):
         moving = fields[component]
         advect = fields[0] * flow_slope(moving, 0)
         advect = advect + fields[1] * flow_slope(moving, 1)
         advect = advect + fields[2] * flow_slope(moving, 2)
-        source = moving - STEP_FLOW * (advect + flow_slope(fields[3], component))
-        relaxed = source
-        for sweep_number in range(SWEEPS):
+        source = moving - STEP_FLOW * (advect + pushes[component])
+
+        def sweep(number, relaxed):
             beside = jnp.zeros_like(relaxed)
             for direction in range(3):
                 beside = beside + flow_beside(relaxed, direction, 1)
                 beside = beside + flow_beside(relaxed, direction, -1)
-            relaxed = (source + IMPLICIT * beside) * (1.0 / (1.0 + 6.0 * IMPLICIT))
-        moved.append(relaxed[flow_margin : flow_margin + flow_chunk])
-
-    pltpu.make_async_copy(level_in, level_in, take_sems.at[0]).wait()
+            return (source + IMPLICIT * beside) * (1.0 / (1.0 + 6.0 * IMPLICIT))
+
+        relaxed = lax.fori_loop(0, SWEEPS, sweep, source)
+        results[component] = relaxed[flow_margin : flow_margin + flow_chunk]
+        return carry
+
+    lax.fori_loop(0, 3, relax, 0)
+
+    pltpu.make_async_copy(stages.at[0], stages.at[0], take_sems.at[0]).wait()
 
     block_rows = 2 * ROWS
 
-    def section(current, target, keep, blend):
-        def one(major, carry):
+    def section(number, carry):
+        later = (number > 0).astype(jnp.float32)
+        latest = (number > 1).astype(jnp.float32)
+        keep = later * 0.75 - latest * (0.75 - 1.0 / 3.0)
+        blend = 1.0 - keep
+
+        def one(major, inner_carry):
             def far_major(step):
                 return lax.rem(major + majors + step, majors)
 
             for start in range(0, body, block_rows):
                 rows = pl.ds(offset + start, block_rows)
-                tall = current[major, pl.ds(start, block_rows + 2 * offset)]
+                tall = stages[number, major, pl.ds(start, block_rows + 2 * offset)]
                 middle = tall[offset : offset + block_rows]
                 low_half = lanes_of(middle.shape) < fine_z
-                whole = {step: current[far_major(step), rows] for step in (-2, -1, 1, 2)}
+                whole = {step: stages[number, far_major(step), rows] for step in (-2, -1, 1, 2)}
                 whole[0] = middle
                 swapped = {step: pltpu.roll(whole[step], fine_z, 1) for step in whole}
 
@@ -636,16 +677,13 @@
                     pace = jnp.abs(speed) * (1.0 / 6.0)
                     rate = rate - weno_flux(bends, near, speed, forward, pace)
                 moved_on = blend * (middle + STEP_FINE * rate)
-                if keep:
-                    moved_on = keep * level_in[major, rows] + moved_on
-                target[major, rows] = moved_on
-            return carry
+                stages[number + 1, major, rows] = keep * stages[0, major, rows] + moved_on
+            return inner_carry
 
         lax.fori_loop(0, majors, one, 0)
-
-    section(level_in, stage_one, 0.0, 1.0)
-    section(stage_one, stage_two, 0.75, 0.25)
-    section(stage_two, stage_one, 1.0 / 3.0, 2.0 / 3.0)
+        return carry
+
+    lax.fori_loop(0, 3, section, 0)
 
     pltpu.make_async_copy(marks_in, marks_in, take_sems.at[2]).wait()
     mark_from = lax.broadcasted_iota(jnp.int32, (LANES, LANES), 0)
@@ -663,7 +701,7 @@
             ).astype(jnp.float32)
             phase = jnp.dot(marks, pick, preferred_element_type=jnp.float32)
             major = part * pairs + pair
-            banded = jnp.where(band > 0.5, stage_one[major, inside], level_in[major, inside])
+            banded = jnp.where(band > 0.5, stages[3, major, inside], stages[0, major, inside])
             shaped[major] = jnp.where(
                 phase > 1.5, SPREAD, jnp.where(phase > 0.5, -SPREAD, banded)
             )
@@ -672,11 +710,11 @@
 
     def x_slope(ref, major):
         here = pltpu.roll(ref[major], fine_z, 1)
-        up = pltpu.roll(ref[(major + 1) % majors], fine_z, 1)
-        down = pltpu.roll(ref[(major + majors - 1) % majors], fine_z, 1)
+        up = pltpu.roll(ref[lax.rem(major + 1, majors)], fine_z, 1)
+        down = pltpu.roll(ref[lax.rem(major + majors - 1, majors)], fine_z, 1)
         return 0.5 * (jnp.where(low_half, here, up) - jnp.where(low_half, down, here))
 
-    for major in range(majors):
+    def steepness(major, carry):
         level = shaped[major]
         slope_x = x_slope(shaped, major)
         slope_y = 0.5 * (along_rows(level, 1) - along_rows(level, -1))
@@ -685,9 +723,16 @@
         normals[0, major] = slope_x * inverse
         normals[1, major] = slope_y * inverse
         normals[2, major] = slope_z * inverse
+        return carry
+
+    lax.fori_loop(0, majors, steepness, 0)
 
     core = slice(mark_margin, mark_margin + fine_chunk)
-    for major in range(majors):
+    fine_from = lax.broadcasted_iota(jnp.int32, (LANES, LANES), 0) % fine_z // 2
+    flow_to = lanes_of((LANES, LANES))
+    folded[...] = jnp.zeros_like(folded)
+
+    def tension(major, carry):
         normal_y, normal_z = normals[1, major], normals[2, major]
         curvature = x_slope(normals.at[0], major)
         curvature = curvature + 0.5 * (along_rows(normal_y, 1) - along_rows(normal_y, -1))
@@ -697,46 +742,41 @@
         level = shaped[major]
         delta_peak = jnp.exp(level * level * (-1.0 / (2.0 * SPREAD * SPREAD)))
         strength = (SURFACE / (SPREAD * 2.5066282746310002)) * curvature * delta_peak
-        lane_spot = slice(major * LANES, (major + 1) * LANES)
-        for direction in range(3):
-            force = (normals[direction, major] * strength)[core]
-            packed[pl.ds(direction * fine_chunk, fine_chunk), lane_spot] = force
-        fraction = (0.5 + 0.5 * jnp.tanh(level * (1.0 / SPREAD)))[core]
-        packed[pl.ds(3 * fine_chunk, fine_chunk), lane_spot] = fraction
-
-    fine_from = lax.broadcasted_iota(jnp.int32, (majors * LANES, LANES), 0)
-    flow_to = lanes_of((majors * LANES, LANES))
-    fold_lanes = (
-        flow_to == (fine_from // LANES) * flow_z + (fine_from % fine_z) // 2
-    ).astype(jnp.float32)
-    folded = jnp.dot(
-        packed[...], fold_lanes, precision=EXACT, preferred_element_type=jnp.float32
-    )
+        terms = [(normals[direction, major] * strength)[core] for direction in range(3)]
+        terms.append((0.5 + 0.5 * jnp.tanh(level * (1.0 / SPREAD)))[core])
+        fold = (flow_to == major * flow_z + fine_from).astype(jnp.float32)
+        folded[...] += jnp.dot(
+            jnp.concatenate(terms, axis=0),
+            fold,
+            precision=EXACT,
+            preferred_element_type=jnp.float32,
+        )
+        return carry
+
+    lax.fori_loop(0, majors, tension, 0)
+
     fold_shape = (4 * flow_chunk, 4 * fine_chunk)
     fold_rows = (
         lanes_of(fold_shape) // 2 == lax.broadcasted_iota(jnp.int32, fold_shape, 0)
     ).astype(jnp.float32)
     means = 0.125 * jnp.dot(
-        fold_rows, folded, precision=EXACT, preferred_element_type=jnp.float32
+        fold_rows, folded[...], precision=EXACT, preferred_element_type=jnp.float32
     )
     for output in range(4):
         mean = means[output * flow_chunk : (output + 1) * flow_chunk]
-        results[output] = moved[output] + STEP_FLOW * mean if output < 3 else mean
-
-    landing = pl.ds(pl.multiple_of(mine * flow_chunk, flow_chunk), flow_chunk)
-    for chunk in range(chunks):
-        push(results.at[chunk // halves], gathered.at[landing], chunk, ring, 3)
+        results[output] = results[output] + STEP_FLOW * mean if output < 3 else mean
+
+    spread_results(False)
     pltpu.make_async_copy(gathered, gathered, take_sems.at[3]).wait()
     turned = gathered[...].T
     outcome = turned[:share]
     for part in range(1, halves):
         outcome = jnp.where(half == part, turned[part * share : (part + 1) * share], outcome)
     out_ref[...] = outcome
-    for condition, copy in sent:
-        if condition is None:
-            copy.wait_send()
-        else:
-            pl.when(condition)(copy.wait_send)
+    pl.when(holder)(lambda: spread_level(True))
+    spread_flow(True)
+    spread_marks(True)
+    spread_results(True)
 
 
 def on_device_bricks(plan, flow_fields, level_set, band_tiles, nozzle_phase):
@@ -762,7 +802,7 @@
     def room(*shape):
         return pltpu.VMEM(shape, jnp.float32)
 
-    copies = 4 * chunks + 6
+    copies = 4 * (chunks + 2)
     result = pl.pallas_call(
         functools.partial(brick_kernel, plan),
         out_shape=jax.ShapeDtypeStruct((flow_x * flow_z, flow_y), jnp.float32),
@@ -777,14 +817,14 @@
             room(fine_x // 2, fine_y, LANES),
             room(fine_y, LANES),
             room(groups, halves, flow_chunk + 2 * ROWS, LANES),
-            room(majors, tall, LANES),
+            room(4, majors, tall, LANES),
             room(halves, body, LANES),
             room(3, majors, body, LANES),
-            room(majors, tall, LANES),
-            room(majors, tall, LANES),
+            room(groups, flow_chunk + 2 * ROWS, LANES),
+            room(3, flow_chunk + 2 * ROWS, LANES),
             room(majors, body, LANES),
             room(3, majors, body, LANES),
-            room(4 * fine_chunk, majors * LANES),
+            room(4 * fine_chunk, LANES),
             room(4, flow_chunk, LANES),
             room(flow_y, LANES),
             pltpu.SemaphoreType.DMA((copies,)),

time: 23.4 us -> 29.8 us (1.27)
  Pallas kernels: 21.8 us -> 28.2 us
    pallas_call x1, Pallas kernels: 21.8 us -> 28.2 us  [on_device_bricks(): pl.pallas_call(functools.partial(brick_kernel, plan), out_shape=jax.Shape...]
where the time goes in v6:
time: 29.8 us; the launch traced here: 29.6 us
  Pallas kernels  28.2 us (95%)
  local copies, waits for them, and re-layouts  1.4 us (5%)
    pallas_call x1, Pallas kernels, on_device_bricks(): pl.pallas_call(functools.partial(brick_kernel, plan), out_shape=jax.Shape...  28.2 us
    reshape x1, local copies, waits for them, and re-layouts, on_device_bricks(): return result.reshape(flow_x, flow_z, flow_y).transpose(1, 0, 2)[None]  1.4 us

profile of v6, /device:TPU:0, one launch (start us, length us, event | category | flops | bytes accessed | tf_op | source)
XLA Modules:
  0.0 29.6 jit_solution(9760528711432549350)
XLA Ops:
  0.0 28.2 %jet_step.1 = f32[64,128]{1,0:T(8,128)} custom-call(f32[32,2,128]{2,1,0:T(2,128)} %bitcast.11, f32[64,4,256]{2,1,0:T(4,128)} %bitcast.9, s32[8,16]{1,0:T(8,128)} %bitcast.12, s32[4,256]{1,0:T(4,128)} %phase_far.1), custom_call_target="tpu_custom_call" | custom-call | tf_op jit(solution)/shard_map/jet_step/pallas_call | solution.py:806
  28.2 1.4 %copy.7 = f32[2,32,128]{2,0,1:T(2,128)} copy(f32[2,32,128]{2,1,0:T(8,128)} %bitcast.10) | data formatting | bytes 65536 | tf_op jit(solution)/shard_map/reshape | solution.py:839

commit v7 on v4

--- a/solution.py
+++ b/solution.py
@@ -262,6 +262,16 @@
 
 def along_rows(block, offset):
     return pltpu.roll(block, (-offset) % block.shape[0], 0)
+
+
+def halves_of(block):
+    top = block.astype(jnp.bfloat16)
+    rest = (block - top.astype(jnp.float32)).astype(jnp.bfloat16)
+    return top, rest
+
+
+def plain_dot(left, right):
+    return jnp.dot(left, right, preferred_element_type=jnp.float32)
 
 
 def inverse_of(block):
@@ -544,20 +554,25 @@
     from_flow = lax.broadcasted_iota(jnp.int32, (LANES, majors * LANES), 0)
     to_fine = lanes_of((LANES, majors * LANES))
     fine_cell = (to_fine // LANES) * flow_z + (to_fine % fine_z) // 2
-    spread_lanes = (from_flow == fine_cell).astype(jnp.float32)
+    spread_lanes = (from_flow == fine_cell).astype(jnp.bfloat16)
     flow_window = flow_chunk + 2 * flow_margin
+    spread_shape = (3 * body, 3 * flow_window)
+    spread_to = lax.broadcasted_iota(jnp.int32, spread_shape, 0)
     spread_rows = (
-        lanes_of((body, flow_window))
-        == lax.broadcasted_iota(jnp.int32, (body, flow_window), 0) // 2
+        lanes_of(spread_shape)
+        == spread_to // body * flow_window
+        + spread_to % body // 2
         + (flow_margin - mark_margin // 2)
-    ).astype(jnp.float32)
+    ).astype(jnp.bfloat16)
+    wide = jnp.zeros((3 * body, majors * LANES), jnp.float32)
+    for piece in halves_of(jnp.concatenate(fields[:3], axis=0)):
+        tall = plain_dot(spread_rows, piece).astype(jnp.bfloat16)
+        wide = wide + plain_dot(tall, spread_lanes)
     for direction in range(3):
-        tall = jnp.dot(
-            spread_rows, fields[direction], precision=EXACT, preferred_element_type=jnp.float32
-        )
-        wide = jnp.dot(tall, spread_lanes, precision=EXACT, preferred_element_type=jnp.float32)
         for major in range(majors):
-            speeds[direction, major] = wide[:, major * LANES : (major + 1) * LANES]
+            speeds[direction, major] = wide[
+                direction * body : (direction + 1) * body, major * LANES : (major + 1) * LANES
+            ]
 
     def flow_beside(block, direction, step):
         if direction == 0:
@@ -617,20 +632,10 @@
 
                 rate = jnp.zeros_like(middle)
                 for direction in range(3):
-                    if direction == 2:
-                        first = along_z(middle, 1, fine_z) - middle
-                        behind = along_z(first, -1, fine_z)
-                        bend = first - behind
-                        bends = [
-                            along_z(bend, step, fine_z) if step else bend
-                            for step in (-2, -1, 0, 1, 2)
-                        ]
-                        near = (behind, first)
-                    else:
-                        cells = [beside(direction, step) for step in range(-3, 4)]
-                        diffs = [cells[i + 1] - cells[i] for i in range(6)]
-                        bends = [diffs[i + 1] - diffs[i] for i in range(5)]
-                        near = (diffs[2], diffs[3])
+                    cells = [beside(direction, step) for step in range(-3, 4)]
+                    diffs = [cells[i + 1] - cells[i] for i in range(6)]
+                    bends = [diffs[i + 1] - diffs[i] for i in range(5)]
+                    near = (diffs[2], diffs[3])
                     speed = speeds[direction, major, pl.ds(start, block_rows)]
                     forward = speed >= 0.0
                     pace = jnp.abs(speed) * (1.0 / 6.0)
@@ -708,17 +713,15 @@
     flow_to = lanes_of((majors * LANES, LANES))
     fold_lanes = (
         flow_to == (fine_from // LANES) * flow_z + (fine_from % fine_z) // 2
-    ).astype(jnp.float32)
-    folded = jnp.dot(
-        packed[...], fold_lanes, precision=EXACT, preferred_element_type=jnp.float32
-    )
+    ).astype(jnp.bfloat16)
+    top, rest = halves_of(packed[...])
+    folded = plain_dot(top, fold_lanes) + plain_dot(rest, fold_lanes)
     fold_shape = (4 * flow_chunk, 4 * fine_chunk)
     fold_rows = (
         lanes_of(fold_shape) // 2 == lax.broadcasted_iota(jnp.int32, fold_shape, 0)
-    ).astype(jnp.float32)
-    means = 0.125 * jnp.dot(
-        fold_rows, folded, precision=EXACT, preferred_element_type=jnp.float32
-    )
+    ).astype(jnp.bfloat16)
+    top, rest = halves_of(folded)
+    means = 0.125 * (plain_dot(fold_rows, top) + plain_dot(fold_rows, rest))
     for output in range(4):
         mean = means[output * flow_chunk : (output + 1) * flow_chunk]
         results[output] = moved[output] + STEP_FLOW * mean if output < 3 else mean

time: 23.4 us -> 22.9 us (0.979)
  Pallas kernels: 21.8 us -> 21.2 us
    pallas_call x1, Pallas kernels: 21.8 us -> 21.2 us  [on_device_bricks(): pl.pallas_call(functools.partial(brick_kernel, plan), out_shape=jax.Shape...]
where the time goes in v7:
time: 22.9 us; the launch traced here: 22.7 us
  Pallas kernels  21.2 us (93%)
  local copies, waits for them, and re-layouts  1.4 us (6%)
    pallas_call x1, Pallas kernels, on_device_bricks(): pl.pallas_call(functools.partial(brick_kernel, plan), out_shape=jax.Shape...  21.2 us
    reshape x1, local copies, waits for them, and re-layouts, on_device_bricks(): return result.reshape(flow_x, flow_z, flow_y).transpose(1, 0, 2)[None]  1.4 us

profile of v7, /device:TPU:0, one launch (start us, length us, event | category | flops | bytes accessed | tf_op | source)
XLA Modules:
  0.0 22.7 jit_solution(17785950644616481404)
XLA Ops:
  0.0 21.2 %jet_step.1 = f32[64,128]{1,0:T(8,128)} custom-call(f32[32,2,128]{2,1,0:T(2,128)} %bitcast.11, f32[64,4,256]{2,1,0:T(4,128)} %bitcast.9, s32[8,16]{1,0:T(8,128)} %bitcast.12, s32[4,256]{1,0:T(4,128)} %phase_far.1), custom_call_target="tpu_custom_call" | custom-call | tf_op jit(solution)/shard_map/jet_step/pallas_call | solution.py:769
  21.3 1.4 %copy.7 = f32[2,32,128]{2,0,1:T(2,128)} copy(f32[2,32,128]{2,1,0:T(8,128)} %bitcast.10) | data formatting | bytes 65536 | tf_op jit(solution)/shard_map/reshape | solution.py:802

commit v8 on v7

--- a/solution.py
+++ b/solution.py
@@ -378,19 +378,17 @@
         )
 
     for chunk in range(chunks):
-        tg, th = chunk // halves, chunk % halves
 
         @pl.when(mine != chunk)
-        def _(tg=tg, th=th):
-            greet(tg, th, ring)
-
-        @pl.when(mine == 0)
-        def _(tg=tg, th=th):
-            greet(tg, th, before)
-
-        @pl.when(mine == last)
-        def _(tg=tg, th=th):
-            greet(tg, th, after)
+        def _(chunk=chunk):
+            greet(chunk // halves, chunk % halves, ring)
+
+    for edge_chunk, beyond in ((0, before), (last, after)):
+
+        @pl.when(mine == edge_chunk)
+        def _(beyond=beyond):
+            for chunk in range(chunks):
+                greet(chunk // halves, chunk % halves, beyond)
 
     @pl.when(holder)
     def _():
@@ -427,112 +425,81 @@
 
     sent = []
 
-    def push(source, target, chunk, ring_to, take, condition=None):
-        tg, th = chunk // halves, chunk % halves
-        slot = len(sent)
+    def entry(source, target, chunk, ring_to, take, slot):
         remote = pltpu.make_async_remote_copy(
             src_ref=source,
             dst_ref=target,
-            send_sem=send_sems.at[slot],
+            send_sem=send_sems.at[take * (chunks + 2) + slot],
             recv_sem=take_sems.at[take],
-            device_id=(tg, th, ring_to),
+            device_id=(chunk // halves, chunk % halves, ring_to),
             device_id_type=MESH,
         )
-        near = ring_to is ring
-        far = mine != chunk if near else None
-        if condition is not None:
-            far = condition if far is None else jnp.logical_and(condition, far)
-        if near:
-            here = mine == chunk
-            if condition is not None:
-                here = jnp.logical_and(condition, here)
-
-            @pl.when(here)
-            def _():
-                pltpu.make_async_copy(source, target, take_sems.at[take]).start()
-
-        if far is None:
-            remote.start()
+
+        def local():
+            pltpu.make_async_copy(source, target, take_sems.at[take]).start()
+
+        return chunk, ring_to is ring, remote, local
+
+    def act(entries, own_group, finish):
+        for chunk, near, remote, local in entries:
+            step = remote.wait_send if finish else remote.start
+            if near and own_group in (None, chunk // halves):
+                pl.when(mine != chunk)(step)
+                if not finish:
+                    pl.when(mine == chunk)(local)
+            else:
+                step()
+
+    def guarded(entries, own_group, finish):
+        if own_group is None:
+            act(entries, own_group, finish)
         else:
-            pl.when(far)(remote.start)
-        sent.append((far, remote))
+            pl.when(group == own_group)(lambda: act(entries, own_group, finish))
+
+    def brick_entries(source, target, chunk_rows, margin, take):
+        entries = []
+        for chunk in range(chunks):
+            start, count, spot = window(chunk, chunks, chunk_rows, margin)
+            rows, landed = pl.ds(start, count), pl.ds(spot, count)
+            entries.append(entry(source(rows), target(landed), chunk, ring, take, chunk))
+        rows = pl.ds(chunks * chunk_rows - margin, margin)
+        landed = pl.ds(0, margin)
+        entries.append(entry(source(rows), target(landed), 0, after, take, chunks))
+        rows, landed = pl.ds(0, margin), pl.ds(margin + chunk_rows, margin)
+        entries.append(entry(source(rows), target(landed), last, before, take, chunks + 1))
+        return entries
 
     major_spot = pl.ds(half * pairs, pairs)
-    for chunk in range(chunks):
-        start, count, spot = window(chunk, chunks, fine_chunk, fine_margin)
-        push(
-            level_turned.at[:, pl.ds(start, count)],
-            level_in.at[major_spot, pl.ds(spot, count)],
-            chunk,
-            ring,
-            0,
-            holder,
-        )
-    push(
-        level_turned.at[:, pl.ds(fine_rows - fine_margin, fine_margin)],
-        level_in.at[major_spot, pl.ds(0, fine_margin)],
+    level_entries = brick_entries(
+        lambda rows: level_turned.at[:, rows],
+        lambda rows: level_in.at[major_spot, rows],
+        fine_chunk,
+        fine_margin,
         0,
-        after,
-        0,
-        holder,
-    )
-    push(
-        level_turned.at[:, pl.ds(0, fine_margin)],
-        level_in.at[major_spot, pl.ds(fine_margin + fine_chunk, fine_margin)],
-        last,
-        before,
-        0,
-        holder,
-    )
-    for chunk in range(chunks):
-        start, count, spot = window(chunk, chunks, flow_chunk, flow_margin)
-        push(
-            flow_turned.at[pl.ds(start, count)],
-            flow_in.at[group, half, pl.ds(spot, count)],
-            chunk,
-            ring,
-            1,
-        )
-    push(
-        flow_turned.at[pl.ds(flow_rows - flow_margin, flow_margin)],
-        flow_in.at[group, half, pl.ds(0, flow_margin)],
-        0,
-        after,
+    )
+    flow_entries = brick_entries(
+        lambda rows: flow_turned.at[rows],
+        lambda rows: flow_in.at[group, half, rows],
+        flow_chunk,
+        flow_margin,
         1,
     )
-    push(
-        flow_turned.at[pl.ds(0, flow_margin)],
-        flow_in.at[group, half, pl.ds(flow_margin + flow_chunk, flow_margin)],
-        last,
-        before,
-        1,
-    )
-    for chunk in range(chunks):
-        start, count, spot = window(chunk, chunks, fine_chunk, mark_margin)
-        push(
-            marks_turned.at[pl.ds(start, count)],
-            marks_in.at[half, pl.ds(spot, count)],
-            chunk,
-            ring,
-            2,
-            group == chunk // halves,
-        )
-    push(
-        marks_turned.at[pl.ds(fine_rows - mark_margin, mark_margin)],
-        marks_in.at[half, pl.ds(0, mark_margin)],
-        0,
-        after,
+    mark_entries = brick_entries(
+        lambda rows: marks_turned.at[rows],
+        lambda rows: marks_in.at[half, rows],
+        fine_chunk,
+        mark_margin,
         2,
-        group == 0,
-    )
-    push(
-        marks_turned.at[pl.ds(0, mark_margin)],
-        marks_in.at[half, pl.ds(mark_margin + fine_chunk, mark_margin)],
-        last,
-        before,
-        2,
-        group == groups - 1,
-    )
+    )
+
+    def first_round(finish):
+        guarded(level_entries, groups - 1, finish)
+        guarded(flow_entries, None, finish)
+        for part in range(groups):
+            picked = [one for one in mark_entries if one[0] // halves == part]
+            guarded(picked, part, finish)
+
+    first_round(False)
 
     body = fine_chunk + 2 * mark_margin
     offset = fine_margin - mark_margin
@@ -727,19 +694,19 @@
         results[output] = moved[output] + STEP_FLOW * mean if output < 3 else mean
 
     landing = pl.ds(pl.multiple_of(mine * flow_chunk, flow_chunk), flow_chunk)
-    for chunk in range(chunks):
-        push(results.at[chunk // halves], gathered.at[landing], chunk, ring, 3)
+    result_entries = [
+        entry(results.at[chunk // halves], gathered.at[landing], chunk, ring, 3, chunk)
+        for chunk in range(chunks)
+    ]
+    act(result_entries, None, False)
+    first_round(True)
+    act(result_entries, None, True)
     pltpu.make_async_copy(gathered, gathered, take_sems.at[3]).wait()
     turned = gathered[...].T
     outcome = turned[:share]
     for part in range(1, halves):
         outcome = jnp.where(half == part, turned[part * share : (part + 1) * share], outcome)
     out_ref[...] = outcome
-    for condition, copy in sent:
-        if condition is None:
-            copy.wait_send()
-        else:
-            pl.when(condition)(copy.wait_send)
 
 
 def on_device_bricks(plan, flow_fields, level_set, band_tiles, nozzle_phase):
@@ -765,7 +732,7 @@
     def room(*shape):
         return pltpu.VMEM(shape, jnp.float32)
 
-    copies = 4 * chunks + 6
+    copies = 4 * (chunks + 2)
     result = pl.pallas_call(
         functools.partial(brick_kernel, plan),
         out_shape=jax.ShapeDtypeStruct((flow_x * flow_z, flow_y), jnp.float32),

time: 22.9 us -> 22.8 us (level)
  no operation moved by 1% of the time
where the time goes in v8:
time: 22.8 us; the launch traced here: 22.6 us
  Pallas kernels  21.2 us (93%)
  local copies, waits for them, and re-layouts  1.4 us (6%)
    pallas_call x1, Pallas kernels, on_device_bricks(): pl.pallas_call(functools.partial(brick_kernel, plan), out_shape=jax.Shape...  21.2 us
    reshape x1, local copies, waits for them, and re-layouts, on_device_bricks(): return result.reshape(flow_x, flow_z, flow_y).transpose(1, 0, 2)[None]  1.4 us

profile of v8, /device:TPU:0, one launch (start us, length us, event | category | flops | bytes accessed | tf_op | source)
XLA Modules:
  0.0 22.6 jit_solution(9507840438685537789)
XLA Ops:
  0.0 21.2 %jet_step.1 = f32[64,128]{1,0:T(8,128)} custom-call(f32[32,2,128]{2,1,0:T(2,128)} %bitcast.11, f32[64,4,256]{2,1,0:T(4,128)} %bitcast.9, s32[8,16]{1,0:T(8,128)} %bitcast.12, s32[4,256]{1,0:T(4,128)} %phase_far.1), custom_call_target="tpu_custom_call" | custom-call | tf_op jit(solution)/shard_map/jet_step/pallas_call | solution.py:736
  21.2 1.4 %copy.7 = f32[2,32,128]{2,0,1:T(2,128)} copy(f32[2,32,128]{2,1,0:T(8,128)} %bitcast.10) | data formatting | bytes 65536 | tf_op jit(solution)/shard_map/reshape | solution.py:769
